TPU v7x, 128 devices: a whole 4x4x4 slice. The times are simulated.
128 devices in a mesh: section: 4 (over x), zone: 32 (over z, y, core).
Axes of the slice: x: 4, y: 4, z: 4, core: 2. Of those that a mesh axis runs over, the one named last changes fastest.
Arguments:
- tiles: bfloat16 [4, 4096, 128, 128], P('section', 'zone'), may hold values from -0.5 to 0.5
- tile_row: int32 [4, 4096], P('section', 'zone'), may hold values from 0 to 19
- tile_col: int32 [4, 4096], P('section', 'zone'), may hold values from 0 to 63, as said below
- tile_live: int32 [4, 4096], P('section', 'zone'), may hold values from 0 to 1, as said below
- block_place: int32 [64], replicated, may hold values from 0 to 63, as said below
- demand: int32 [4, 81920, 128], P('section', 'zone'), may hold values from 0 to 15
- flow_cost: float32 [4, 8192], P('section', 'zone'), may hold values from -6 to 6
- stock_cost: float32 [4, 81920], P('section', 'zone'), may hold values from 0.1 to 1
- flows: float32 [4, 8192, 128], P('section', 'zone'), may hold values from 0 to 1
- stock: float32 [4, 81920, 128], P('section', 'zone'), may hold values from 0 to 2
- duals: float32 [4, 81920, 128], P('section', 'zone'), may hold values from -6 to 6
Outputs:
- flows_out: float32 [4, 8192, 128], P('section', 'zone')
- stock_out: float32 [4, 81920, 128], P('section', 'zone')
- duals_out: float32 [4, 81920, 128], P('section', 'zone')
Inputs may be any that keep to these rules, and one draw needn't show every extreme that they name: `tile_col`: flow block ids. For each phase and zone band, at most 4 live slots name flow blocks whose position // 2 is one given band; in each phase one band receives exactly 4 such slots from every zone band. `tile_live`: live flags of the slots, with the counts described for tile_col. `block_place`: A permutation of the flow blocks.
All inputs are finite; a program needn't handle non-finite values.
Results may differ from a plain program's by a relative error of at most 0.019.
Values may be sent and summed in bfloat16 or wider, within the bound.
A program may use at most 128 MiB of HBM per device.

v0:
```python
import jax
import jax.numpy as jnp
from jax import lax
from jax.sharding import PartitionSpec as P

ITERS = 2


STEP_PRIMAL = 0.25
STEP_DUAL = 0.25


def from_behind(value, axis, by):
    size = lax.axis_size(axis)
    return lax.ppermute(value, axis, [(i, (i + by) % size) for i in range(size)])


def per_device(
    tiles,
    tile_row,
    tile_col,
    tile_live,
    block_place,
    demand,
    flow_cost,
    stock_cost,
    flows,
    stock,
    duals,
):
    phase_count, slot_count, tile_size, unused_size = tiles.shape
    scenarios = flows.shape[2]
    zone_count = lax.axis_size("zone")
    blocks_total = block_place.shape[0]
    block_local = blocks_total // zone_count
    band_tiles = duals.shape[1] // tile_size
    width_flat = tile_size * scenarios
    alive = tile_live == 1
    position = block_place[tile_col]
    demand_rhs = demand.astype(jnp.float32) * 0.25
    phase_ids = jnp.arange(phase_count, dtype=jnp.int32)[:, None]
    block_ids = jnp.where(alive, position, -1)
    row_live = jnp.where(alive, tile_row, band_tiles)
    for iteration in range(ITERS):
        dual_half = duals.astype(jnp.bfloat16).reshape(
            phase_count, band_tiles, tile_size, scenarios
        )
        dual_picked = jnp.take_along_axis(dual_half, tile_row[:, :, None, None], axis=1)
        partial_value = jnp.einsum(
            "snij,snic->snjc", tiles, dual_picked, preferred_element_type=jnp.float32
        )
        partial_value = partial_value.astype(jnp.bfloat16).reshape(
            phase_count, slot_count, width_flat
        )
        shifted = jnp.where(block_ids >= 0, block_ids, -1)
        shifted = jnp.where(shifted < lax.axis_size("zone") * block_local, shifted, -1)

        def one_phase(values, segment_ids):
            return jax.ops.segment_sum(
                values.astype(jnp.float32),
                segment_ids,
                num_segments=lax.axis_size("zone") * block_local,
            )

        summed_blocks = jax.vmap(one_phase)(partial_value, shifted)
        summed = lax.psum_scatter(
            jnp.transpose(summed_blocks, (1, 0, 2)), "zone", scatter_dimension=0, tiled=True
        )
        pulled = jnp.transpose(summed, (1, 0, 2))
        pulled = pulled.reshape(phase_count, block_local * tile_size, scenarios)
        dual_edge = from_behind(duals, "section", -1)
        dual_after = jnp.concatenate([duals[1:], dual_edge], axis=0)
        new_flows = jnp.maximum(flows - STEP_PRIMAL * (flow_cost[:, :, None] - pulled), 0.0)
        new_stock = jnp.maximum(
            stock - STEP_PRIMAL * (stock_cost[:, :, None] - dual_after + duals), 0.0
        )
        flows_bar = (2.0 * new_flows - flows).astype(jnp.bfloat16)
        stock_bar = 2.0 * new_stock - stock
        gathered = lax.all_gather(flows_bar, "zone", axis=1, tiled=True).reshape(
            phase_count, blocks_total, tile_size, scenarios
        )
        flow_picked = jnp.take_along_axis(gathered, position[:, :, None, None], axis=1)
        products = jnp.einsum(
            "snij,snjc->snic", tiles, flow_picked, preferred_element_type=jnp.float32
        )
        pushed = (
            jnp.zeros((phase_count, band_tiles, tile_size, scenarios), jnp.float32)
            .at[phase_ids, row_live]
            .add(products, mode="drop")
        )
        pushed = pushed.reshape(phase_count, band_tiles * tile_size, scenarios)
        stock_edge = from_behind(stock_bar, "section", 1)
        stock_before = jnp.concatenate([stock_edge, stock_bar[:-1]], axis=0)
        duals = duals + STEP_DUAL * (demand_rhs - (pushed + stock_before - stock_bar))
        flows = new_flows
        stock = new_stock
    return (flows, stock, duals)


def solution(mesh):
    in_specs = (
        P("section", "zone", None, None),
        P("section", "zone"),
        P("section", "zone"),
        P("section", "zone"),
        P(),
        P("section", "zone", None),
        P("section", "zone"),
        P("section", "zone"),
        P("section", "zone", None),
        P("section", "zone", None),
        P("section", "zone", None),
    )
    out_specs = (P("section", "zone", None), P("section", "zone", None), P("section", "zone", None))
    return jax.shard_map(
        per_device, mesh=mesh, in_specs=in_specs, out_specs=out_specs, check_vma=False
    )
```

profile of v0, /device:TPU:1, one launch (start us, length us, event | category | flops | bytes accessed | tf_op | source)
XLA Modules:
  0.0 547.1 jit_solution(18323352815189189794)
XLA Ops:
  15.3 23.1 %collective-permute-done = f32[1,2560,128]{2,1,0:T(8,128)} collective-permute-done((f32[1,2560,128]{2,1,0:T(8,128)}, f32[1,2560,128]{2,1,0:T(8,128)}, u32[]{:S(2)}, u32[]{:S(2)}) %collective-permute-start) | collective-permute-done | bytes 1310752 | tf_op jit(solution)/shard_map/ppermute | solution.py:15
  38.4 4.0 multiply_subtract_fusion.1
  45.4 8.4 %convert_bitcast_fusion.1 = f32[128,128,128]{1,2,0:T(8,128)} fusion(bf16[1,128,128,128]{3,2,1,0:T(8,128)(2,1)} %param.15, bf16[128,128,128]{2,1,0:T(8,128)(2,1)} %gather_fusion.1, pred[128]{0:T(512)(128)(4,1)S(1)} %and_bitcast_fusion.1), kind=kOutput, calls=%fused_computation.10 | convolution fusion | flops 543162368 | bytes 16777344 | tf_op jit(solution)/shard_map/snij,snic->snjc/dot_general | solution.py:49
  53.8 9.4 %copy.35 = f32[128,128,128]{0,2,1:T(8,128)} copy(f32[128,128,128]{1,2,0:T(8,128)} %convert_bitcast_fusion.1) | data formatting | bytes 16777216 | tf_op jit(solution)/shard_map/vmap()/convert_element_type | solution.py:60
  63.2 9.0 %copy.36 = f32[128,16384]{1,0:T(8,128)} copy(f32[128,16384]{0,1:T(8,128)} %bitcast.163) | data formatting | bytes 16777216 | tf_op jit(solution)/shard_map/vmap()/convert_element_type | solution.py:60
  72.2 15.1 %scatter_custom_fusion.2 = f32[64,16384]{1,0:T(8,128)} fusion(s32[128]{0:T(128)S(1)} %fusion.51, f32[128,16384]{1,0:T(8,128)} %copy.36, f32[]{:T(128)} %constant.3.clone.1), kind=kCustom, calls=%fused_computation.39 | custom fusion | flops 2097152 | bytes 4194816 | tf_op jit(solution)/shard_map/vmap()/scatter-add | solution.py:59
  88.6 114.6 %all-reduce.6.cloned.1.call-done = f32[64,1,16384]{2,0,1:T(8,128)} async-done(((f32[64,1,16384]{2,0,1:T(8,128)}), f32[64,1,16384]{2,0,1:T(8,128)}) %all-reduce.6.cloned.1.call-update) | async-done | bytes 4194320
  207.1 42.9 %all-gather.3.cloned.1.call-done = bf16[1,8192,128]{2,1,0:T(8,128)(2,1)} async-done(((bf16[1,256,128]{2,1,0:T(8,128)(2,1)}), bf16[1,8192,128]{2,1,0:T(8,128)(2,1)}) %all-gather.3.cloned.1.call-update) | async-done | bytes 2097168 | tf_op jit(solution)/shard_map/all_gather | solution.py:79
  250.1 4.6 gather_fusion.2
  254.7 9.9 %fusion.20 = f32[128,128,128]{1,2,0:T(8,128)} fusion(bf16[1,128,128,128]{3,2,1,0:T(8,128)(2,1)} %param.15, bf16[128,128,128]{2,1,0:T(8,128)(2,1)} %gather_fusion.2, pred[128]{0:T(512)(128)(4,1)S(1)} %and_bitcast_fusion), kind=kOutput, calls=%fused_computation.31 | convolution fusion | flops 538968064 | bytes 16777344 | tf_op jit(solution)/shard_map/snij,snjc->snic/dot_general | solution.py:83
  264.6 9.0 %copy.38 = f32[128,128,128]{2,1,0:T(8,128)} copy(f32[128,128,128]{1,2,0:T(8,128)} %fusion.20) | data formatting | bytes 16777216 | tf_op jit(solution)/shard_map/snij,snjc->snic/dot_general | solution.py:83
  273.8 17.0 %scatter_fusion = f32[20,128,128]{2,1,0:T(8,128)S(1)} fusion(f32[20,128,128]{2,1,0:T(8,128)S(1)} %broadcast.166.clone, s32[128]{0:T(128)S(1)} %fusion.50, f32[128,128,128]{2,1,0:T(8,128)} %copy.38), kind=kCustom, calls=%fused_computation.5 | custom fusion | flops 2097152 | bytes 25166336 | tf_op jit(solution)/shard_map/scatter-add | solution.py:89
  296.9 8.4 %convert_bitcast_fusion = f32[128,128,128]{1,2,0:T(8,128)} fusion(bf16[1,128,128,128]{3,2,1,0:T(8,128)(2,1)} %param.15, bf16[128,128,128]{2,1,0:T(8,128)(2,1)} %gather_fusion.3, pred[128]{0:T(512)(128)(4,1)S(1)} %copy-done.9), kind=kOutput, calls=%fused_computation.9 | convolution fusion | flops 543162368 | bytes 16777344 | tf_op jit(solution)/shard_map/snij,snic->snjc/dot_general | solution.py:49
  305.3 9.4 %copy.40 = f32[128,128,128]{0,2,1:T(8,128)} copy(f32[128,128,128]{1,2,0:T(8,128)} %convert_bitcast_fusion) | data formatting | bytes 16777216 | tf_op jit(solution)/shard_map/vmap()/convert_element_type | solution.py:60
  314.7 9.0 %copy.41 = f32[128,16384]{1,0:T(8,128)} copy(f32[128,16384]{0,1:T(8,128)} %bitcast.164) | data formatting | bytes 16777216 | tf_op jit(solution)/shard_map/vmap()/convert_element_type | solution.py:60
  323.7 15.1 %scatter_custom_fusion.3 = f32[64,16384]{1,0:T(8,128)} fusion(s32[128]{0:T(128)} %copy-done.14, f32[128,16384]{1,0:T(8,128)} %copy.41, f32[]{:T(128)} %constant.3.clone.1), kind=kCustom, calls=%fused_computation.37 | custom fusion | flops 2097152 | bytes 4194816 | tf_op jit(solution)/shard_map/vmap()/scatter-add | solution.py:59
  338.8 110.8 %all-reduce.8.cloned.1.call-done = f32[64,1,16384]{2,0,1:T(8,128)} async-done(((f32[64,1,16384]{2,0,1:T(8,128)}), f32[64,1,16384]{2,0,1:T(8,128)}) %all-reduce.8.cloned.1.call-update) | async-done | bytes 4194320
  454.1 27.4 %collective-permute-done.2 = f32[1,2560,128]{2,1,0:T(8,128)S(1)} collective-permute-done((f32[1,2560,128]{2,1,0:T(8,128)S(1)}, f32[1,2560,128]{2,1,0:T(8,128)S(1)}, u32[]{:S(2)}, u32[]{:S(2)}) %collective-permute-start.2) | collective-permute-done | bytes 1310752 | tf_op jit(solution)/shard_map/ppermute | solution.py:15
  484.7 11.1 %all-gather.5.cloned.1.call-done = bf16[1,8192,128]{2,1,0:T(8,128)(2,1)} async-done(((bf16[1,256,128]{2,1,0:T(8,128)(2,1)}), bf16[1,8192,128]{2,1,0:T(8,128)(2,1)}) %all-gather.5.cloned.1.call-update) | async-done | bytes 2097168 | tf_op jit(solution)/shard_map/all_gather | solution.py:79
  495.8 4.8 gather_fusion.4
  500.6 9.9 %fusion.29 = f32[128,128,128]{1,2,0:T(8,128)} fusion(bf16[1,128,128,128]{3,2,1,0:T(8,128)(2,1)} %param.15, bf16[128,128,128]{2,1,0:T(8,128)(2,1)} %gather_fusion.4, pred[128]{0:T(512)(128)(4,1)S(1)} %copy-done.11), kind=kOutput, calls=%fused_computation.32 | convolution fusion | flops 538968064 | bytes 16777344 | tf_op jit(solution)/shard_map/snij,snjc->snic/dot_general | solution.py:83
  510.5 9.0 %copy.43 = f32[128,128,128]{2,1,0:T(8,128)} copy(f32[128,128,128]{1,2,0:T(8,128)} %fusion.29) | data formatting | bytes 16777216 | tf_op jit(solution)/shard_map/snij,snjc->snic/dot_general | solution.py:83
  519.6 17.0 %scatter_fusion.1 = f32[20,128,128]{2,1,0:T(8,128)S(1)} fusion(f32[20,128,128]{2,1,0:T(8,128)S(1)} %broadcast.166, s32[128]{0:T(128)S(1)} %copy-done.13, f32[128,128,128]{2,1,0:T(8,128)} %copy.43), kind=kCustom, calls=%fused_computation.6 | custom fusion | flops 2097152 | bytes 25166336 | tf_op jit(solution)/shard_map/scatter-add | solution.py:89
  536.7 3.7 fusion.45
  (73 shorter events, 29.6 us)
Async XLA Ops:
  7.2 4.1 copy-start
  7.2 196.1 %all-reduce.6.cloned.1.call-start = ((), (), s32[]{:S(2)}) async-start(), calls=%async_computation.2 | async-start | bytes 8388608
  7.2 31.1 %collective-permute-start = (f32[1,2560,128]{2,1,0:T(8,128)}, f32[1,2560,128]{2,1,0:T(8,128)}, u32[]{:S(2)}, u32[]{:S(2)}) collective-permute-start(f32[1,2560,128]{2,1,0:T(8,128)} %param.25), channel_id=1, source_target_pairs={{0,96},{32,0},{64,32},{96,64},{1,97},{33,1},{65,33},{97,65},{2,98}... | collective-permute-start | bytes 3932168 | tf_op jit(solution)/shard_map/ppermute | solution.py:15
  15.3 30.1 %copy-start.8 = (pred[128]{0:T(512)(128)(4,1)}, pred[128]{0:T(512)(128)(4,1)S(1)}, u32[]{:S(2)}) copy-start(pred[128]{0:T(512)(128)(4,1)S(1)} %and_bitcast_fusion.1) | copy-start | bytes 388
  15.3 56.9 %copy-start.14 = (s32[128]{0:T(128)}, s32[128]{0:T(128)S(1)}, u32[]{:S(2)}) copy-start(s32[128]{0:T(128)S(1)} %fusion.51) | copy-start | bytes 1540
  42.3 162.9 %copy-start.3 = (f32[1,2560,128]{2,1,0:T(8,128)}, f32[1,2560,128]{2,1,0:T(8,128)S(1)}, u32[]{:S(2)}) copy-start(f32[1,2560,128]{2,1,0:T(8,128)S(1)} %get-tuple-element.11) | copy-start | bytes 3932164
  72.2 15.2 %copy-start.15 = (u32[128]{0:T(128)S(1)}, u32[128]{0:T(128)}, u32[]{:S(2)}) copy-start(u32[128]{0:T(128)} %constant.66) | copy-start | bytes 1540
  72.2 132.3 %copy-start.4 = (f32[1,256,128]{2,1,0:T(8,128)S(1)}, f32[1,256,128]{2,1,0:T(8,128)}, u32[]{:S(2)}) copy-start(f32[1,256,128]{2,1,0:T(8,128)} %param.23) | copy-start | bytes 393220
  72.2 132.3 %copy-start.6 = (f32[1,256]{1,0:T(1,128)S(1)}, f32[1,256]{1,0:T(1,128)}, u32[]{:S(2)}) copy-start(f32[1,256]{1,0:T(1,128)} %param.21) | copy-start | bytes 3076
  87.3 162.8 %all-gather.3.cloned.1.call-start = ((), (), s32[]{:S(2)}) async-start(), calls=%async_computation | async-start | bytes 2162688 | tf_op jit(solution)/shard_map/all_gather | solution.py:79
  205.2 244.4 %all-reduce.8.cloned.1.call-start = ((), (), s32[]{:S(2)}) async-start(), calls=%async_computation.3 | async-start | bytes 8388608
  205.3 85.5 %collective-permute-start.1 = (f32[1,2560,128]{2,1,0:T(8,128)S(1)}, f32[1,2560,128]{2,1,0:T(8,128)}, u32[]{:S(2)}, u32[]{:S(2)}) collective-permute-start(f32[1,2560,128]{2,1,0:T(8,128)S(1)} %get-tuple-element.11), channel_id=1, source_target_pairs={{0,32},{32,64},{64,96},{96,0},{1,33},{33,65},{65,97},{97,1},{2,34}... | collective-permute-start | bytes 3932168 | tf_op jit(solution)/shard_map/ppermute | solution.py:15
  207.1 47.6 %copy-start.5 = (s32[1024]{0:T(1024)}, s32[1024]{0:T(1024)S(1)}, u32[]{:S(2)}) copy-start(s32[1024]{0:T(1024)S(1)} %pad_clamp_fusion) | copy-start | bytes 12292
  207.1 47.6 %copy-start.10 = (pred[128]{0:T(512)(128)(4,1)}, pred[128]{0:T(512)(128)(4,1)S(1)}, u32[]{:S(2)}) copy-start(pred[128]{0:T(512)(128)(4,1)S(1)} %and_bitcast_fusion) | copy-start | bytes 388
  207.1 66.6 %copy-start.12 = (s32[128]{0:T(128)}, s32[128]{0:T(128)S(1)}, u32[]{:S(2)}) copy-start(s32[128]{0:T(128)S(1)} %fusion.50) | copy-start | bytes 1540
  293.8 3.1 copy-start.9
  323.7 127.2 %copy-start.7 = (f32[1,256]{1,0:T(1,128)S(1)}, f32[1,256]{1,0:T(1,128)}, u32[]{:S(2)}) copy-start(f32[1,256]{1,0:T(1,128)} %param.21) | copy-start | bytes 3076
  323.7 157.9 %copy-start.2 = (f32[1,2560,128]{2,1,0:T(8,128)S(1)}, f32[1,2560,128]{2,1,0:T(8,128)}, u32[]{:S(2)}) copy-start(f32[1,2560,128]{2,1,0:T(8,128)} %get-tuple-element.12) | copy-start | bytes 3932164
  338.8 157.0 %all-gather.5.cloned.1.call-start = ((), (), s32[]{:S(2)}) async-start(), calls=%async_computation.1 | async-start | bytes 2162688 | tf_op jit(solution)/shard_map/all_gather | solution.py:79
  451.7 29.9 %collective-permute-start.2 = (f32[1,2560,128]{2,1,0:T(8,128)S(1)}, f32[1,2560,128]{2,1,0:T(8,128)S(1)}, u32[]{:S(2)}, u32[]{:S(2)}) collective-permute-start(f32[1,2560,128]{2,1,0:T(8,128)S(1)} %get-tuple-element.10), channel_id=1, source_target_pairs={{0,96},{32,0},{64,32},{96,64},{1,97},{33,1},{65,33},{97,65},{2,98}... | collective-permute-start | bytes 3932168 | tf_op jit(solution)/shard_map/ppermute | solution.py:15
  483.5 53.1 %collective-permute-start.3 = (f32[1,2560,128]{2,1,0:T(8,128)}, f32[1,2560,128]{2,1,0:T(8,128)}, u32[]{:S(2)}, u32[]{:S(2)}) collective-permute-start(f32[1,2560,128]{2,1,0:T(8,128)} %get-tuple-element.7), channel_id=1, source_target_pairs={{0,32},{32,64},{64,96},{96,0},{1,33},{33,65},{65,97},{97,1},{2,34}... | collective-permute-start | bytes 3932168 | tf_op jit(solution)/shard_map/ppermute | solution.py:15
  495.8 4.8 copy-start.11
  510.5 9.1 %copy-start.13 = (s32[128]{0:T(128)S(1)}, s32[128]{0:T(128)}, u32[]{:S(2)}) copy-start(s32[128]{0:T(128)} %copy-done.12) | copy-start | bytes 1540
  519.6 20.8 %copy-start.1 = (s32[64]{0:T(128)S(1)}, s32[64]{0:T(128)}, u32[]{:S(2)}) copy-start(s32[64]{0:T(128)} %param.19) | copy-start | bytes 772
Sparse Core Ops, SparseCore 0:
  87.4 115.7 all-reduce.5
  206.1 43.9 all-gather.2
  338.9 110.6 all-reduce.7
  451.8 43.9 all-gather.4
where the time goes:
time: 553 us; the launch traced here: 547 us
  waiting for transfers between devices  330 us (60%)
  other arithmetic  81.8 us (15%)
  local copies, waits for them, and re-layouts  74.9 us (14%)
  matrix products  36.6 us (7%)
  between operations  14.9 us (3%)
  starting transfers between devices  8.97 us (2%)
    unnamed x6, waiting for transfers between devices  225 us
    all_gather x2, waiting for transfers between devices, per_device(): lax.all_gather(flows_bar, 'zone', axis=1, tiled=True)  54 us
    ppermute x4, waiting for transfers between devices, from_behind(): lax.ppermute(value, axis, [(i, (i + by) % size) for i in range(size)])  50.5 us
    convert_element_type x4, local copies, waits for them, and re-layouts, one_phase(): values.astype(jnp.float32)  36.8 us
    scatter-add x2, other arithmetic, per_device(): pushed = jnp.zeros((phase_count, band_tiles, tile_size, scenarios), jnp.f...  34.1 us
    scatter-add x3, other arithmetic, one_phase(): jax.ops.segment_sum(values.astype(jnp.float32), segment_ids, num_segments...  30.2 us
    dot_general x2, matrix products, per_device(): jnp.einsum('snij,snjc->snic', tiles, flow_picked, preferred_element_type=...  19.8 us
    dot_general x2, local copies, waits for them, and re-layouts, per_device(): jnp.einsum('snij,snjc->snic', tiles, flow_picked, preferred_element_type=...  18 us
  transfers between devices with their start and end apart: 8, of which 6 were waited for; matrix products, arithmetic and copies ran while one was open for 16% of the time, Pallas kernels for 0%

commit v1 on v0

v1 whole, which is shorter than its diff:
```python
import functools

import jax
import jax.numpy as jnp
from jax import lax
from jax.experimental import pallas as pl
from jax.experimental.pallas import tpu as pltpu
from jax.sharding import PartitionSpec as P

ITERS = 2
STEP_PRIMAL = 0.25
STEP_DUAL = 0.25

SIDE = 4
CAP = 4
TILE = 128
OFFSETS = (2, 1, 3)
MESH = pl.DeviceIdType.MESH

F32 = jnp.float32
BF16 = jnp.bfloat16


def lanes_to_rows(row):
    return jnp.transpose(jnp.broadcast_to(row, (TILE, TILE)))


def prepare(place_ref, tile_row_ref, tile_col_ref, tile_live_ref, table_ref):
    along = lax.broadcasted_iota(jnp.int32, (TILE, TILE), 1).astype(F32)
    down = lax.broadcasted_iota(jnp.int32, (TILE, TILE), 0).astype(F32)
    zone_tile = tile_row_ref[...].astype(F32)
    column = tile_col_ref[...].astype(F32)
    live = tile_live_ref[...] == 1

    def total(array):
        return jnp.sum(array, axis=0, keepdims=True)

    position = total(jnp.where(down == column, lanes_to_rows(place_ref[...].astype(F32)), 0.0))
    band = jnp.where(live, jnp.floor(position * 0.5), 1000.0)
    offset = position - 2.0 * jnp.floor(position * 0.5)
    rank = total(jnp.where((lanes_to_rows(band) == band) & (down < along), 1.0, 0.0))
    entry = jnp.where(live, band * CAP + rank, 1000.0)
    code = along[0:1] + 128.0 * zone_tile + 4096.0 * (offset + 1.0)
    packed = total(jnp.where(lanes_to_rows(entry) == along, lanes_to_rows(code), 0.0))
    block = jnp.floor(packed * (1.0 / 4096.0))
    rest = packed - 4096.0 * block
    row = jnp.floor(rest * (1.0 / 128.0))
    slot = rest - 128.0 * row
    which = jnp.where(block == 0.0, 2.0, block - 1.0)

    row_down = lanes_to_rows(row)
    spot = total(jnp.where((row_down < row) | ((row_down == row) & (down < along)), 1.0, 0.0))
    spot_down = lanes_to_rows(spot)
    order = total(jnp.where(spot_down == along, down, 0.0))
    sorted_row = total(jnp.where(spot_down == along, row_down, 0.0))
    before = total(jnp.where(spot_down == along - 1.0, row_down, 0.0))
    keep = jnp.where((sorted_row == before) & (along[0:1] > 0.0), 1.0, 0.0)
    upto = total(jnp.where(row_down <= along, 1.0, 0.0))
    count = total(jnp.where(row_down == along, 1.0, 0.0))
    last = jnp.maximum(upto - 1.0, 0.0)
    some = jnp.where(count > 0.0, 1.0, 0.0)
    rows = (slot, row, which, order, keep, last, some, some)
    for number, value in enumerate(rows):
        table_ref[number : number + 1, :] = value.astype(jnp.int32)


def steps(
    table,
    tiles_hbm,
    demand_hbm,
    flow_cost_hbm,
    stock_cost_hbm,
    flows_hbm,
    stock_hbm,
    duals_hbm,
    flows_out,
    stock_out,
    duals_out,
    tiles,
    demand,
    flow_cost,
    stock_cost,
    flows,
    stock,
    duals,
    dual_turned,
    dual_send,
    dual_next,
    bar_send,
    bar_before,
    pair_send,
    pair_got,
    far_send,
    far_got,
    far_own,
    near_send,
    near_got,
    blocks,
    products,
    running,
    load_sem,
    store_sem,
    x_send_sem,
    x_got_sem,
    sum_send_sem,
    sum_got_sem,
    block_send_sem,
    block_got_sem,
):
    section = lax.axis_index("section")
    me = lax.axis_index("zone")
    core = me % 2
    chip_y = (me // 2) % SIDE
    chip_z = me // (2 * SIDE)
    far = chip_z * (1 - core) + chip_y * core
    near = chip_y * (1 - core) + chip_z * core

    def zone_of(far_at, near_at, core_at):
        z_at = far_at * (1 - core_at) + near_at * core_at
        y_at = near_at * (1 - core_at) + far_at * core_at
        return (z_at * SIDE + y_at) * 2 + core_at

    pair = zone_of(near, far, 1 - core)
    far_peers = [zone_of((far + off) % SIDE, near, core) for off in OFFSETS]
    near_peers = [zone_of(far, (near + off) % SIDE, core) for off in OFFSETS]
    section_after = (section + 1) % SIDE
    section_before = (section + SIDE - 1) % SIDE

    loads = [
        pltpu.make_async_copy(source, target, load_sem.at[number])
        for number, (source, target) in enumerate(
            (
                (duals_hbm.at[0], duals),
                (tiles_hbm.at[0], tiles),
                (stock_cost_hbm, stock_cost),
                (flow_cost_hbm, flow_cost),
                (stock_hbm.at[0], stock),
                (demand_hbm.at[0], demand),
                (flows_hbm.at[0], flows),
            )
        )
    ]
    for load in loads:
        load.start()

    barrier = pltpu.get_barrier_semaphore()
    partners = [(section, peer) for peer in [pair] + far_peers + near_peers]
    partners += [(section_after, me), (section_before, me)]
    for partner in partners:
        pl.semaphore_signal(barrier, inc=1, device_id=partner, device_id_type=MESH)
    pl.semaphore_wait(barrier, len(partners))

    zone_tiles = duals.shape[0] // TILE
    chunks = x_send_sem.shape[1]
    chunk_tiles = zone_tiles // chunks
    chunk_rows = chunk_tiles * TILE

    def rows_of(tile):
        return pl.ds(pl.multiple_of(tile * TILE, TILE), TILE)

    def remote(source, target, send_sem, got_sem, device):
        return pltpu.make_async_remote_copy(
            src_ref=source,
            dst_ref=target,
            send_sem=send_sem,
            recv_sem=got_sem,
            device_id=device,
            device_id_type=MESH,
        )

    def dual_copy(it, chunk):
        rows = pl.ds(chunk * chunk_rows, chunk_rows)
        return remote(
            dual_send.at[rows],
            dual_next.at[it, rows],
            x_send_sem.at[0, chunk],
            x_got_sem.at[it, 0, chunk],
            (section_before, me),
        )

    def bar_copy(it, chunk):
        rows = pl.ds(chunk * chunk_rows, chunk_rows)
        return remote(
            bar_send.at[rows],
            bar_before.at[it, rows],
            x_send_sem.at[1, chunk],
            x_got_sem.at[it, 1, chunk],
            (section_after, me),
        )

    def store_dual(chunk):
        rows = pl.ds(chunk * chunk_rows, chunk_rows)
        return pltpu.make_async_copy(duals.at[rows], duals_out.at[0, rows], store_sem.at[1 + chunk])

    def store_stock(chunk):
        rows = pl.ds(chunk * chunk_rows, chunk_rows)
        return pltpu.make_async_copy(
            stock.at[rows], stock_out.at[0, rows], store_sem.at[1 + chunks + chunk]
        )

    store_flows = pltpu.make_async_copy(flows, flows_out.at[0], store_sem.at[0])

    def send_duals(chunk, value_of, it):
        def turn(step, carry):
            tile = chunk * chunk_tiles + step
            half = value_of(tile).astype(BF16)
            dual_send[rows_of(tile), :] = half
            dual_turned[tile] = jnp.transpose(half)
            return carry

        lax.fori_loop(0, chunk_tiles, turn, 0, unroll=2)
        dual_copy(it, chunk).start()

    def pull_band(band):
        first = jnp.zeros((TILE, TILE), F32)
        second = jnp.zeros((TILE, TILE), F32)
        for number in range(CAP):
            entry = band * CAP + number
            which = table[2, entry]
            product = jnp.dot(
                dual_turned[table[1, entry]],
                tiles[table[0, entry]],
                preferred_element_type=F32,
            )
            first = first + jnp.where(which == 0, product, 0.0)
            second = second + jnp.where(which == 1, product, 0.0)
        return first, second

    def push_band(it, band):
        held = blocks[it, band]
        for number in range(CAP):
            entry = band * CAP + number
            which = table[2, entry]
            chosen = jnp.where(
                which == 0,
                held[:TILE],
                jnp.where(which == 1, held[TILE:], jnp.zeros((TILE, TILE), BF16)),
            )
            products[entry] = jnp.dot(tiles[table[0, entry]], chosen, preferred_element_type=F32)

    def pair_copy(it, part):
        return remote(
            pair_send.at[part],
            pair_got.at[it, part],
            sum_send_sem.at[0, part],
            sum_got_sem.at[it, 0, part],
            (section, pair),
        )

    def far_copy(it, part):
        return remote(
            far_send.at[part],
            far_got.at[it, part],
            sum_send_sem.at[1, part],
            sum_got_sem.at[it, 1, part],
            (section, far_peers[part]),
        )

    def near_copy(it, part):
        return remote(
            near_send.at[part],
            near_got.at[it, part],
            sum_send_sem.at[2, part],
            sum_got_sem.at[it, 2, part],
            (section, near_peers[part]),
        )

    def pull_for_pair(it, part):
        group = (near + (OFFSETS + (0,))[part]) % SIDE

        def one(step, carry):
            first, second = pull_band(zone_of(group, step, 1 - core))
            pair_send[part, step, :, :TILE] = first.astype(BF16)
            pair_send[part, step, :, TILE:] = second.astype(BF16)
            return carry

        lax.fori_loop(0, SIDE, one, 0, unroll=2)
        pair_copy(it, part).start()

    def pull_own(it, part):
        group = (far + (OFFSETS + (0,))[part]) % SIDE
        pair_copy(it, part).wait_recv()

        def one(step, carry):
            first, second = pull_band(zone_of(group, step, core))
            first = first + pair_got[it, part, step, :, :TILE].astype(F32)
            second = second + pair_got[it, part, step, :, TILE:].astype(F32)
            if part < len(OFFSETS):
                far_send[part, step, :, :TILE] = first.astype(BF16)
                far_send[part, step, :, TILE:] = second.astype(BF16)
            else:
                far_own[step, :, :TILE] = first
                far_own[step, :, TILE:] = second
            return carry

        lax.fori_loop(0, SIDE, one, 0, unroll=2)
        if part < len(OFFSETS):
            far_copy(it, part).start()

    def update_stock(it, chunk):
        dual_copy(it, chunk).wait_recv()

        def one(step, carry):
            tile = chunk * chunk_tiles + step
            rows = rows_of(tile)
            cost = lanes_to_rows(stock_cost[:, rows])
            dual = duals[rows, :]
            held = stock[rows, :]
            after = dual_next[it, rows, :].astype(F32)
            fresh = jnp.maximum(held - STEP_PRIMAL * (cost - after + dual), 0.0)
            bar = 2.0 * fresh - held
            stock[rows, :] = fresh
            bar_send[rows, :] = bar.astype(BF16)
            duals[rows, :] = dual + STEP_DUAL * (demand[rows, :].astype(F32) * 0.25 + bar)
            return carry

        lax.fori_loop(0, chunk_tiles, one, 0, unroll=2)
        bar_copy(it, chunk).start()
        if it == ITERS - 1:
            store_stock(chunk).start()

    def block_copy(it, band, send_number, device):
        return remote(
            blocks.at[it, band],
            blocks.at[it, band],
            block_send_sem.at[send_number],
            block_got_sem.at[it, band],
            (section, device),
        )

    loads[0].wait()
    for chunk in range(chunks):
        send_duals(chunk, lambda tile: duals[rows_of(tile), :], 0)
    loads[1].wait()

    for it in range(ITERS):
        pull_for_pair(it, 0)
        pull_for_pair(it, 1)
        pull_own(it, 0)
        pull_for_pair(it, 2)
        pull_own(it, 1)
        pull_for_pair(it, 3)
        pull_own(it, 2)
        pull_own(it, 3)
        if it == 0:
            for load in loads[2:]:
                load.wait()
        update_stock(it, 0)
        for part in range(len(OFFSETS)):
            far_copy(it, part).wait_recv()

        def near_sum(at):
            total = far_own[at]
            for part in range(len(OFFSETS)):
                total = total + far_got[it, part, at].astype(F32)
            return total

        for part, off in enumerate(OFFSETS):
            near_send[part] = near_sum((near + off) % SIDE).astype(BF16)
            near_copy(it, part).start()
        pulled = near_sum(near)
        update_stock(it, 1)
        for part in range(len(OFFSETS)):
            near_copy(it, part).wait_recv()
        for part in range(len(OFFSETS)):
            pulled = pulled + near_got[it, part].astype(F32)

        for block in range(flows.shape[0] // TILE):
            rows = pl.ds(block * TILE, TILE)
            cost = lanes_to_rows(flow_cost[:, rows])
            here = jnp.transpose(pulled[:, block * TILE : (block + 1) * TILE])
            held = flows[rows, :]
            fresh = jnp.maximum(held - STEP_PRIMAL * (cost - here), 0.0)
            flows[rows, :] = fresh
            blocks[it, me, rows, :] = (2.0 * fresh - held).astype(BF16)
        sends = []

        def send_block(band, device):
            copy = block_copy(it, band, len(sends), device)
            copy.start()
            sends.append(copy)

        def got(band):
            return block_copy(it, band, 0, pair)

        for peer in near_peers:
            send_block(me, peer)
        send_block(me, pair)
        for peer in far_peers:
            send_block(me, peer)
        if it == ITERS - 1:
            store_flows.start()
        push_band(it, me)
        update_stock(it, 2)
        for peer in near_peers:
            got(peer).wait_recv()
            for device in far_peers:
                send_block(peer, device)
            send_block(peer, pair)
        for peer in near_peers:
            push_band(it, peer)
        got(pair).wait_recv()
        push_band(it, pair)
        update_stock(it, 3)
        for off in OFFSETS:
            at = (far + off) % SIDE
            for back in (0,) + OFFSETS:
                band = zone_of(at, (near + back) % SIDE, core)
                got(band).wait_recv()
                send_block(band, pair)

            def far_push(step, carry):
                push_band(it, zone_of(at, step, core))
                return carry

            lax.fori_loop(0, SIDE, far_push, 0, unroll=2)
        update_stock(it, 4)
        for number, off in enumerate((0,) + OFFSETS):
            at = (near + off) % SIDE
            backs = OFFSETS if off == 0 else (0,) + OFFSETS
            for back in backs:
                got(zone_of(at, (far + back) % SIDE, 1 - core)).wait_recv()

            def pair_push(step, carry):
                push_band(it, zone_of(at, (far + step) % SIDE, 1 - core))
                return carry

            lax.fori_loop(1 if off == 0 else 0, SIDE, pair_push, 0, unroll=1)

        def accumulate(step, value):
            value = jnp.where(table[4, step] == 1, value, 0.0) + products[table[3, step]]
            running[step] = value
            return value

        lax.fori_loop(
            0, CAP * SIDE * SIDE * 2, accumulate, jnp.zeros((TILE, TILE), F32), unroll=4
        )
        for chunk in range(chunks):
            bar_copy(it, chunk).wait_recv()
            dual_copy(it, chunk).wait_send()

            def dual_value(tile):
                rows = rows_of(tile)
                pushed = jnp.where(table[6, tile] == 1, running[table[5, tile]], 0.0)
                pushed = pushed + bar_before[it, rows, :].astype(F32)
                value = duals[rows, :] - STEP_DUAL * pushed
                duals[rows, :] = value
                return value

            if it < ITERS - 1:
                send_duals(chunk, dual_value, it + 1)
            else:

                def finish(step, carry):
                    dual_value(chunk * chunk_tiles + step)
                    return carry

                lax.fori_loop(0, chunk_tiles, finish, 0, unroll=2)
                store_dual(chunk).start()
        for chunk in range(chunks):
            bar_copy(it, chunk).wait_send()
        for part in range(SIDE):
            pair_copy(it, part).wait_send()
        for part in range(len(OFFSETS)):
            far_copy(it, part).wait_send()
            near_copy(it, part).wait_send()
        for copy in sends:
            copy.wait_send()
    store_flows.wait()
    for chunk in range(chunks):
        store_stock(chunk).wait()
        store_dual(chunk).wait()


def per_device(
    tiles,
    tile_row,
    tile_col,
    tile_live,
    block_place,
    demand,
    flow_cost,
    stock_cost,
    flows,
    stock,
    duals,
):
    slots = tiles.shape[1]
    zones = duals.shape[1]
    zone_tiles = zones // TILE
    own_flows = flows.shape[1]
    bands = SIDE * SIDE * 2
    others = len(OFFSETS)
    chunks = 5
    place_row = jnp.pad(block_place, (0, TILE - block_place.shape[0])).reshape(1, TILE)
    vmem = pl.BlockSpec(memory_space=pltpu.VMEM)
    anywhere = pl.BlockSpec(memory_space=pl.ANY)
    table = pl.pallas_call(
        prepare,
        out_shape=jax.ShapeDtypeStruct((8, TILE), jnp.int32),
        in_specs=[vmem] * 4,
        out_specs=vmem,
        name="slot_order",
    )(place_row, tile_row, tile_col, tile_live)
    return pl.pallas_call(
        steps,
        out_shape=(
            jax.ShapeDtypeStruct(flows.shape, F32),
            jax.ShapeDtypeStruct(stock.shape, F32),
            jax.ShapeDtypeStruct(duals.shape, F32),
        ),
        in_specs=[pl.BlockSpec(memory_space=pltpu.SMEM)] + [anywhere] * 7,
        out_specs=(anywhere,) * 3,
        scratch_shapes=[
            pltpu.VMEM((slots, TILE, TILE), BF16),
            pltpu.VMEM((zones, TILE), jnp.int32),
            pltpu.VMEM((1, own_flows), F32),
            pltpu.VMEM((1, zones), F32),
            pltpu.VMEM((own_flows, TILE), F32),
            pltpu.VMEM((zones, TILE), F32),
            pltpu.VMEM((zones, TILE), F32),
            pltpu.VMEM((zone_tiles, TILE, TILE), BF16),
            pltpu.VMEM((zones, TILE), BF16),
            pltpu.VMEM((ITERS, zones, TILE), BF16),
            pltpu.VMEM((zones, TILE), BF16),
            pltpu.VMEM((ITERS, zones, TILE), BF16),
            pltpu.VMEM((SIDE, SIDE, TILE, own_flows), BF16),
            pltpu.VMEM((ITERS, SIDE, SIDE, TILE, own_flows), BF16),
            pltpu.VMEM((others, SIDE, TILE, own_flows), BF16),
            pltpu.VMEM((ITERS, others, SIDE, TILE, own_flows), BF16),
            pltpu.VMEM((SIDE, TILE, own_flows), F32),
            pltpu.VMEM((others, TILE, own_flows), BF16),
            pltpu.VMEM((ITERS, others, TILE, own_flows), BF16),
            pltpu.VMEM((ITERS, bands, own_flows, TILE), BF16),
            pltpu.VMEM((bands * CAP, TILE, TILE), F32),
            pltpu.VMEM((bands * CAP, TILE, TILE), F32),
            pltpu.SemaphoreType.DMA((7,)),
            pltpu.SemaphoreType.DMA((1 + 2 * chunks,)),
            pltpu.SemaphoreType.DMA((2, chunks)),
            pltpu.SemaphoreType.DMA((ITERS, 2, chunks)),
            pltpu.SemaphoreType.DMA((3, SIDE)),
            pltpu.SemaphoreType.DMA((ITERS, 3, SIDE)),
            pltpu.SemaphoreType.DMA((bands - 1,)),
            pltpu.SemaphoreType.DMA((ITERS, bands)),
        ],
        compiler_params=pltpu.CompilerParams(
            collective_id=0, has_side_effects=True, vmem_limit_bytes=58 * 2**20
        ),
        name="both_steps",
    )(table, tiles, demand, flow_cost, stock_cost, flows, stock, duals)


def solution(mesh):
    in_specs = (
        P("section", "zone", None, None),
        P("section", "zone"),
        P("section", "zone"),
        P("section", "zone"),
        P(),
        P("section", "zone", None),
        P("section", "zone"),
        P("section", "zone"),
        P("section", "zone", None),
        P("section", "zone", None),
        P("section", "zone", None),
    )
    out_specs = (P("section", "zone", None), P("section", "zone", None), P("section", "zone", None))
    return jax.shard_map(
        per_device, mesh=mesh, in_specs=in_specs, out_specs=out_specs, check_vma=False
    )
```

time: 553 us -> 85.2 us (0.15)
  waiting for transfers between devices: 330 us -> 0 us
  other arithmetic: 81.8 us -> 0 us
  Pallas kernels: 0 us -> 77.6 us
  local copies, waits for them, and re-layouts: 74.9 us -> 6.36 us
  matrix products: 36.6 us -> 0 us
  between operations: 14.9 us -> 0.64 us
  starting transfers between devices: 8.97 us -> 0 us
    unnamed x6 -> x0, waiting for transfers between devices: 225 us -> none
    pallas_call x0 -> x2, Pallas kernels: none -> 77.6 us  [the longest x1 75.7 us: per_device(): pl.pallas_call(steps, out_shape=(jax.ShapeDtypeStruct(flows.shape, F32),...]
    scatter-add x5 -> x0, other arithmetic: 64.2 us -> none  [the longest x2 34.1 us: per_device(): pushed = jnp.zeros((phase_count, band_tiles, tile_size, scenarios), jnp.f...]
    all_gather x2 -> x0, waiting for transfers between devices: 54 us -> none  [per_device(): lax.all_gather(flows_bar, 'zone', axis=1, tiled=True)]
    ppermute x4 -> x0, waiting for transfers between devices: 50.5 us -> none  [from_behind(): lax.ppermute(value, axis, [(i, (i + by) % size) for i in range(size)])]
    convert_element_type x4 -> x0, local copies, waits for them, and re-layouts: 36.8 us -> none  [one_phase(): values.astype(jnp.float32)]
    dot_general x4 -> x0, matrix products: 36.6 us -> none  [the longest x2 19.8 us: per_device(): jnp.einsum('snij,snjc->snic', tiles, flow_picked, preferred_element_type=...]
    dot_general x2 -> x0, local copies, waits for them, and re-layouts: 18 us -> none  [per_device(): jnp.einsum('snij,snjc->snic', tiles, flow_picked, preferred_element_type=...]
  transfers between devices with their start and end apart: 8 -> 0, of which waited for: 6 -> 0; matrix products, arithmetic and copies ran while one was open for 16% -> 0% of each run, Pallas kernels for 0% -> 0%
where the time goes in v1:
time: 85.2 us; the launch traced here: 84.6 us
  Pallas kernels  77.6 us (91%)
  local copies, waits for them, and re-layouts  6.36 us (7%)
    pallas_call x1, Pallas kernels, per_device(): pl.pallas_call(steps, out_shape=(jax.ShapeDtypeStruct(flows.shape, F32),...  75.7 us
    unnamed x5, local copies, waits for them, and re-layouts  5.19 us
    pallas_call x1, Pallas kernels, per_device(): pl.pallas_call(prepare, out_shape=jax.ShapeDtypeStruct((8, TILE), jnp.int...  1.85 us

profile of v1, /device:TPU:1, one launch (start us, length us, event | category | flops | bytes accessed | tf_op | source)
XLA Modules:
  0.0 84.6 jit_solution(17291568512766767904)
XLA Ops:
  0.6 1.2 %pad_bitcast_fusion.place_ref = s32[1,128]{1,0:T(1,128)} fusion(s32[64]{0:T(128)} %param.15), kind=kLoop, calls=%fused_computation | loop fusion | bytes 768 | tf_op jit(solution)/shard_map/reshape | solution.py:495
  1.8 1.9 %slot_order.1.table = s32[8,128]{1,0:T(8,128)} custom-call(s32[1,128]{1,0:T(1,128)} %pad_bitcast_fusion.place_ref, s32[1,128]{1,0:T(1,128)} %tile_row_ref.1, s32[1,128]{1,0:T(1,128)} %tile_col_ref.1, s32[1,128]{1,0:T(1,128)} %tile_live_ref.1), custom_call_target="tpu_custom_call" | custom-call | tf_op jit(solution)/shard_map/slot_order/pallas_call | solution.py:498
  3.7 75.7 %both_steps.1 = (f32[1,256,128]{2,1,0:T(8,128)}, f32[1,2560,128]{2,1,0:T(8,128)}, f32[1,2560,128]{2,1,0:T(8,128)}) custom-call(s32[8,128]{1,0:T(8,128)} %slot_order.1.table, bf16[1,128,128,128]{3,2,1,0:T(8,128)(2,1)} %tiles_hbm.1, s32[1,2560,128]{2,1,0:T(8,128)} %demand_hbm.1, f32[1,256]{1,0:T(1,128)} %flow_cost_hbm.1, f32[1,2560]{1,0:T(1,128)} %stock_cost_hbm.1, ...), custom_call_target="tpu_custom_call" | custom-call | tf_op jit(solution)/shard_map/both_steps/pallas_call | solution.py:505
  79.4 1.6 %copy.17 = f32[1,256,128]{2,1,0:T(8,128)} copy(f32[1,256,128]{2,1,0:T(8,128)} %get-tuple-element.6) | data formatting | bytes 262144
  80.9 0.0 copy-start
  80.9 2.6 %copy.18 = f32[1,2560,128]{2,1,0:T(8,128)} copy(f32[1,2560,128]{2,1,0:T(8,128)} %get-tuple-element.7) | data formatting | bytes 2621440
  83.5 0.0 copy-done
  83.5 1.1 %copy.19 = f32[1,2560,128]{2,1,0:T(8,128)} copy(f32[1,2560,128]{2,1,0:T(8,128)S(1)} %copy-done) | data formatting | bytes 2621440
Async XLA Ops:
  80.9 2.6 %copy-start = (f32[1,2560,128]{2,1,0:T(8,128)S(1)}, f32[1,2560,128]{2,1,0:T(8,128)}, u32[]{:S(2)}) copy-start(f32[1,2560,128]{2,1,0:T(8,128)} %get-tuple-element.8) | copy-start | bytes 3932164

commit v2 on v1

v2 whole, which is shorter than its diff:
```python
import functools

import jax
import jax.numpy as jnp
from jax import lax
from jax.experimental import pallas as pl
from jax.experimental.pallas import tpu as pltpu
from jax.sharding import PartitionSpec as P

ITERS = 2
STEP_PRIMAL = 0.25
STEP_DUAL = 0.25

SIDE = 4
CAP = 4
TILE = 128
NEAR_OFFSETS = (2, 1, 3)
FAR_OFFSETS = (3, 2, 1)
MESH = pl.DeviceIdType.MESH

F32 = jnp.float32
BF16 = jnp.bfloat16


def lanes_to_rows(row):
    return jnp.transpose(jnp.broadcast_to(row, (TILE, row.shape[1])))


def prepare(place_ref, tile_row_ref, tile_col_ref, tile_live_ref, table_ref):
    along = lax.broadcasted_iota(jnp.int32, (TILE, TILE), 1)
    down = lax.broadcasted_iota(jnp.int32, (TILE, TILE), 0)
    live = tile_live_ref[...] == 1

    def total(array):
        return jnp.sum(array, axis=0, keepdims=True)

    place = lanes_to_rows(place_ref[...])
    position = total(jnp.where(down[: place.shape[0]] == tile_col_ref[...], place, 0))
    band = jnp.where(live, position >> 1, 1000)
    rank = total(jnp.where((lanes_to_rows(band) == band) & (down < along), 1, 0))
    entry = jnp.where(live, band * CAP + rank, 1000)
    code = along[0:1] + 128 * tile_row_ref[...] + 4096 * ((position & 1) + 1)
    packed = total(jnp.where(lanes_to_rows(entry) == along, lanes_to_rows(code), 0))
    slot = packed & 127
    row = (packed >> 7) & 31
    block = packed >> 12
    which = jnp.where(block == 0, 2, block - 1)

    row_down = lanes_to_rows(row)
    spot = total(jnp.where((row_down < row) | ((row_down == row) & (down < along)), 1, 0))
    spot_down = lanes_to_rows(spot)
    order = total(jnp.where(spot_down == along, down, 0))
    sorted_row = total(jnp.where(spot_down == along, row_down, 0))
    before = total(jnp.where(spot_down == along - 1, row_down, 0))
    keep = jnp.where((sorted_row == before) & (along[0:1] > 0), 1, 0)
    upto = total(jnp.where(row_down <= along, 1, 0))
    count = total(jnp.where(row_down == along, 1, 0))
    some = jnp.where(count > 0, 1, 0)
    rows = (slot, row, which, order, keep, upto - 1, some, some)
    for number, value in enumerate(rows):
        table_ref[number : number + 1, :] = jnp.clip(value, 0, TILE - 1)


def steps(
    place_hbm,
    tile_row_hbm,
    tile_col_hbm,
    tile_live_hbm,
    tiles_hbm,
    demand_hbm,
    flow_cost_hbm,
    stock_cost_hbm,
    flows_hbm,
    stock_hbm,
    duals_hbm,
    flows_out,
    stock_out,
    duals_out,
    place,
    tile_row,
    tile_col,
    tile_live,
    table_made,
    table,
    tiles,
    demand,
    flow_cost,
    stock_cost,
    cost_turned,
    dual_turned,
    dual_send,
    dual_next,
    bar_send,
    bar_before,
    pair_send,
    pair_got,
    far_send,
    far_got,
    far_own,
    near_send,
    near_got,
    blocks,
    products,
    running,
    load_sem,
    x_send_sem,
    x_got_sem,
    pair_send_sem,
    pair_got_sem,
    far_send_sem,
    far_got_sem,
    near_send_sem,
    near_got_sem,
    block_send_sem,
    block_got_sem,
):
    flows, stock, duals = flows_out.at[0], stock_out.at[0], duals_out.at[0]
    section = lax.axis_index("section")
    me = lax.axis_index("zone")
    core = me % 2
    chip_y = (me // 2) % SIDE
    chip_z = me // (2 * SIDE)
    far = chip_z * (1 - core) + chip_y * core
    near = chip_y * (1 - core) + chip_z * core

    def zone_of(far_at, near_at, core_at):
        far_at, near_at = far_at % SIDE, near_at % SIDE
        z_at = far_at * (1 - core_at) + near_at * core_at
        y_at = near_at * (1 - core_at) + far_at * core_at
        return (z_at * SIDE + y_at) * 2 + core_at

    def own_zone(far_step, near_step):
        return zone_of(far + far_step, near + near_step, core)

    def pair_zone(far_step, near_step):
        return zone_of(near + far_step, far + near_step, 1 - core)

    pair = pair_zone(0, 0)
    far_peers = [own_zone(off, 0) for off in FAR_OFFSETS]
    near_peers = [own_zone(0, off) for off in NEAR_OFFSETS]
    section_after = (section + 1) % SIDE
    section_before = (section + SIDE - 1) % SIDE

    loads = [
        pltpu.make_async_copy(source, target, load_sem.at[number])
        for number, (source, target) in enumerate(
            (
                (place_hbm, place),
                (tile_row_hbm, tile_row),
                (tile_col_hbm, tile_col),
                (tile_live_hbm, tile_live),
                (duals_hbm.at[0], duals),
                (tiles_hbm.at[0], tiles),
                (stock_cost_hbm, stock_cost),
                (flow_cost_hbm, flow_cost),
                (stock_hbm.at[0], stock),
                (demand_hbm.at[0], demand),
                (flows_hbm.at[0], flows),
                (table_made, table),
            )
        )
    ]
    for load in loads[:-1]:
        load.start()

    barrier = pltpu.get_barrier_semaphore()
    partners = [(section, peer) for peer in [pair] + far_peers + near_peers]
    partners += [(section_after, me), (section_before, me)]
    for partner in partners:
        pl.semaphore_signal(barrier, inc=1, device_id=partner, device_id_type=MESH)

    zone_tiles = duals.shape[0] // TILE
    chunks = x_send_sem.shape[1]
    chunk_tiles = zone_tiles // chunks
    chunk_rows = chunk_tiles * TILE

    def rows_of(tile):
        return pl.ds(pl.multiple_of(tile * TILE, TILE), TILE)

    def loop(count, body, unroll=1):
        def step(number, carry):
            body(number)
            return carry

        lax.fori_loop(0, count, step, 0, unroll=unroll)

    def remote(source, target, send_sem, got_sem, device):
        return pltpu.make_async_remote_copy(
            src_ref=source,
            dst_ref=target,
            send_sem=send_sem,
            recv_sem=got_sem,
            device_id=device,
            device_id_type=MESH,
        )

    def dual_copy(it, chunk):
        rows = pl.ds(chunk * chunk_rows, chunk_rows)
        return remote(
            dual_send.at[rows],
            dual_next.at[it, rows],
            x_send_sem.at[0, chunk],
            x_got_sem.at[it, 0, chunk],
            (section_before, me),
        )

    def bar_copy(it, chunk):
        rows = pl.ds(chunk * chunk_rows, chunk_rows)
        return remote(
            bar_send.at[rows],
            bar_before.at[it, rows],
            x_send_sem.at[1, chunk],
            x_got_sem.at[it, 1, chunk],
            (section_after, me),
        )

    def turn(tile, value):
        half = value.astype(BF16)
        dual_send[rows_of(tile), :] = half
        dual_turned[tile] = jnp.transpose(half)

    def pull_band(band):
        first = jnp.zeros((TILE, TILE), F32)
        second = jnp.zeros((TILE, TILE), F32)
        for number in range(CAP):
            entry = band * CAP + number
            which = table[2, entry]
            product = jnp.dot(
                dual_turned[table[1, entry]],
                tiles[table[0, entry]],
                preferred_element_type=F32,
            )
            first = first + jnp.where(which == 0, product, 0.0)
            second = second + jnp.where(which == 1, product, 0.0)
        return first, second

    def push_band(it, band):
        held = blocks[it, band]
        for number in range(CAP):
            entry = band * CAP + number
            which = table[2, entry]
            chosen = jnp.where(
                which == 0,
                held[:TILE],
                jnp.where(which == 1, held[TILE:], jnp.zeros((TILE, TILE), BF16)),
            )
            products[entry] = jnp.dot(tiles[table[0, entry]], chosen, preferred_element_type=F32)

    def pair_copy(it, part):
        return remote(
            pair_send.at[part],
            pair_got.at[it, part],
            pair_send_sem.at[part],
            pair_got_sem.at[it, part],
            (section, pair),
        )

    def far_copy(it, part, number):
        return remote(
            far_send.at[part, number],
            far_got.at[it, part, number],
            far_send_sem.at[part, number],
            far_got_sem.at[it, part, number],
            (section, far_peers[number]),
        )

    def near_copy(it, part):
        return remote(
            near_send.at[part],
            near_got.at[it, part],
            near_send_sem.at[part],
            near_got_sem.at[it, part],
            (section, near_peers[part]),
        )

    def pull_for_pair(it, part):
        def one(number):
            band = pair_zone(SIDE - 1 - number, (NEAR_OFFSETS + (0,))[part])
            first, second = pull_band(band)
            pair_send[part, number, :, :TILE] = first.astype(BF16)
            pair_send[part, number, :, TILE:] = second.astype(BF16)

        loop(SIDE, one, 2)
        pair_copy(it, part).start()

    def pull_own(it, part):
        pair_copy(it, part).wait_recv()
        for number in range(SIDE):
            band = own_zone(SIDE - 1 - number, (NEAR_OFFSETS + (0,))[part])
            first, second = pull_band(band)
            first = first + pair_got[it, part, number, :, :TILE].astype(F32)
            second = second + pair_got[it, part, number, :, TILE:].astype(F32)
            if number < len(FAR_OFFSETS):
                far_send[part, number, :, :TILE] = first.astype(BF16)
                far_send[part, number, :, TILE:] = second.astype(BF16)
            else:
                far_own[part, :, :TILE] = first
                far_own[part, :, TILE:] = second
        for number in range(len(FAR_OFFSETS)):
            far_copy(it, part, number).start()

    def far_sum(it, part):
        for number in range(len(FAR_OFFSETS)):
            far_copy(it, part, number).wait_recv()
        total = far_own[part]
        for number in range(len(FAR_OFFSETS)):
            total = total + far_got[it, part, number].astype(F32)
        return total

    def pass_to_near(it, part):
        near_send[part] = far_sum(it, part).astype(BF16)
        near_copy(it, part).start()

    def update_stock(it, chunk):
        dual_copy(it, chunk).wait_recv()

        def one(step):
            rows = rows_of(chunk * chunk_tiles + step)
            dual = duals[rows, :]
            held = stock[rows, :]
            after = dual_next[it, rows, :].astype(F32)
            fresh = jnp.maximum(held - STEP_PRIMAL * (cost_turned[rows, :] - after + dual), 0.0)
            bar = 2.0 * fresh - held
            stock[rows, :] = fresh
            bar_send[rows, :] = bar.astype(BF16)
            duals[rows, :] = dual + STEP_DUAL * (demand[rows, :].astype(F32) * 0.25 + bar)

        loop(chunk_tiles, one, 2)
        bar_copy(it, chunk).start()

    def block_copy(it, band, number, device):
        return remote(
            blocks.at[it, band],
            blocks.at[it, band],
            block_send_sem.at[number],
            block_got_sem.at[it, band],
            (section, device),
        )

    for load in loads[:4]:
        load.wait()
    prepare(place, tile_row, tile_col, tile_live, table_made)
    loads[-1].start()
    pl.semaphore_wait(barrier, len(partners))
    loads[4].wait()
    for chunk in range(chunks):
        def first_turn(step):
            tile = chunk * chunk_tiles + step
            turn(tile, duals[rows_of(tile), :])

        loop(chunk_tiles, first_turn, 2)
        dual_copy(0, chunk).start()
    loads[6].wait()

    def turn_cost(tile):
        rows = rows_of(tile)
        cost_turned[rows, :] = lanes_to_rows(stock_cost[:, rows])

    loop(zone_tiles, turn_cost, 2)
    loads[-1].wait()
    loads[5].wait()
    for load in loads[7:-1]:
        load.wait()

    def iteration(it):
        pull_for_pair(it, 0)
        pull_for_pair(it, 1)
        pull_own(it, 0)
        pull_for_pair(it, 2)
        pull_own(it, 1)
        pull_for_pair(it, 3)
        pull_own(it, 2)
        pull_own(it, 3)
        update_stock(it, 0)
        for part in range(len(NEAR_OFFSETS)):
            pass_to_near(it, part)
        pulled = far_sum(it, len(NEAR_OFFSETS))
        update_stock(it, 1)
        for part in range(len(NEAR_OFFSETS)):
            near_copy(it, part).wait_recv()
        for part in range(len(NEAR_OFFSETS)):
            pulled = pulled + near_got[it, part].astype(F32)

        for block in range(flows.shape[0] // TILE):
            rows = pl.ds(block * TILE, TILE)
            cost = lanes_to_rows(flow_cost[:, rows])
            here = jnp.transpose(pulled[:, block * TILE : (block + 1) * TILE])
            held = flows[rows, :]
            fresh = jnp.maximum(held - STEP_PRIMAL * (cost - here), 0.0)
            flows[rows, :] = fresh
            blocks[it, me, rows, :] = (2.0 * fresh - held).astype(BF16)

        def got(band):
            block_copy(it, band, 0, pair).wait_recv()

        near_order = (1, 3, 2)
        far_order = (1, 3, 2)
        for number, step in enumerate(near_order):
            block_copy(it, me, number, own_zone(0, step)).start()
        block_copy(it, me, 3, pair).start()
        for number, step in enumerate(far_order):
            block_copy(it, me, 4 + number, own_zone(step, 0)).start()
        push_band(it, me)
        update_stock(it, 2)
        for place_in, near_step in enumerate(near_order):
            band = own_zone(0, near_step)
            got(band)
            for number, step in enumerate(far_order):
                block_copy(it, band, 7 + 4 * place_in + number, own_zone(step, 0)).start()
            block_copy(it, band, 10 + 4 * place_in, pair).start()
        loop(SIDE - 1, lambda step: push_band(it, own_zone(0, step + 1)))
        for near_step in (0,) + near_order:
            got(pair_zone(0, near_step))
        loop(SIDE, lambda step: push_band(it, pair_zone(0, step)), 2)
        update_stock(it, 3)

        def near_of(step):
            return step + (step // 2) * (1 - 2 * (step % 2))

        def own_arrivals(step):
            for number, far_step in enumerate(far_order):
                band = own_zone(far_step, near_of(step))
                got(band)
                block_copy(it, band, 19 + 3 * step + number, pair).start()
            for far_step in far_order:
                push_band(it, own_zone(far_step, near_of(step)))

        def pair_arrivals(step):
            for far_step in far_order:
                got(pair_zone(far_step, near_of(step)))
            for far_step in far_order:
                push_band(it, pair_zone(far_step, near_of(step)))

        def both_arrivals(step):
            own_arrivals(step + 1)
            pair_arrivals(step)

        own_arrivals(0)
        update_stock(it, 4)
        loop(SIDE - 1, both_arrivals)
        pair_arrivals(SIDE - 1)

        def accumulate(step, value):
            value = jnp.where(table[4, step] == 1, value, 0.0) + products[table[3, step]]
            running[step] = value
            return value

        zero = jnp.zeros((TILE, TILE), F32)
        lax.fori_loop(0, products.shape[0], accumulate, zero, unroll=4)
        for chunk in range(chunks):
            bar_copy(it, chunk).wait_recv()
            dual_copy(it, chunk).wait_send()

            def dual_step(step):
                tile = chunk * chunk_tiles + step
                rows = rows_of(tile)
                pushed = jnp.where(table[6, tile] == 1, running[table[5, tile]], 0.0)
                pushed = pushed + bar_before[it, rows, :].astype(F32)
                value = duals[rows, :] - STEP_DUAL * pushed
                duals[rows, :] = value
                turn(tile, value)

            loop(chunk_tiles, dual_step, 2)

            @pl.when(it < ITERS - 1)
            def _():
                dual_copy(it + 1, chunk).start()

        for chunk in range(chunks):
            bar_copy(it, chunk).wait_send()
        for part in range(SIDE):
            pair_copy(it, part).wait_send()
        for part in range(len(NEAR_OFFSETS)):
            near_copy(it, part).wait_send()
        for part in range(SIDE):
            for number in range(len(FAR_OFFSETS)):
                far_copy(it, part, number).wait_send()
        loop(block_send_sem.shape[0], lambda number: block_copy(it, me, number, pair).wait_send())

    loop(ITERS, iteration)


def per_device(
    tiles,
    tile_row,
    tile_col,
    tile_live,
    block_place,
    demand,
    flow_cost,
    stock_cost,
    flows,
    stock,
    duals,
):
    slots = tiles.shape[1]
    zones = duals.shape[1]
    zone_tiles = zones // TILE
    own_flows = flows.shape[1]
    bands = SIDE * SIDE * 2
    others = SIDE - 1
    chunks = 5
    place_row = block_place.reshape(1, -1)
    anywhere = pl.BlockSpec(memory_space=pl.ANY)
    vmem = pl.BlockSpec(memory_space=pltpu.VMEM)
    results = (flows, stock, duals)
    operands = (place_row, tile_row, tile_col, tile_live)
    operands += (tiles, demand, flow_cost, stock_cost, flows, stock, duals)
    results = pl.pallas_call(
        steps,
        out_shape=tuple(pltpu.VMEM(result.shape, F32) for result in results),
        in_specs=[anywhere] * len(operands),
        out_specs=(vmem,) * len(results),
        scratch_shapes=[
            pltpu.VMEM(place_row.shape, jnp.int32),
            pltpu.VMEM((1, slots), jnp.int32),
            pltpu.VMEM((1, slots), jnp.int32),
            pltpu.VMEM((1, slots), jnp.int32),
            pltpu.VMEM((8, TILE), jnp.int32),
            pltpu.SMEM((8, TILE), jnp.int32),
            pltpu.VMEM((slots, TILE, TILE), BF16),
            pltpu.VMEM((zones, TILE), jnp.int32),
            pltpu.VMEM((1, own_flows), F32),
            pltpu.VMEM((1, zones), F32),
            pltpu.VMEM((zones, TILE), F32),
            pltpu.VMEM((zone_tiles, TILE, TILE), BF16),
            pltpu.VMEM((zones, TILE), BF16),
            pltpu.VMEM((ITERS, zones, TILE), BF16),
            pltpu.VMEM((zones, TILE), BF16),
            pltpu.VMEM((ITERS, zones, TILE), BF16),
            pltpu.VMEM((SIDE, SIDE, TILE, own_flows), BF16),
            pltpu.VMEM((ITERS, SIDE, SIDE, TILE, own_flows), BF16),
            pltpu.VMEM((SIDE, others, TILE, own_flows), BF16),
            pltpu.VMEM((ITERS, SIDE, others, TILE, own_flows), BF16),
            pltpu.VMEM((SIDE, TILE, own_flows), F32),
            pltpu.VMEM((others, TILE, own_flows), BF16),
            pltpu.VMEM((ITERS, others, TILE, own_flows), BF16),
            pltpu.VMEM((ITERS, bands, own_flows, TILE), BF16),
            pltpu.VMEM((bands * CAP, TILE, TILE), F32),
            pltpu.VMEM((bands * CAP, TILE, TILE), F32),
            pltpu.SemaphoreType.DMA((12,)),
            pltpu.SemaphoreType.DMA((2, chunks)),
            pltpu.SemaphoreType.DMA((ITERS, 2, chunks)),
            pltpu.SemaphoreType.DMA((SIDE,)),
            pltpu.SemaphoreType.DMA((ITERS, SIDE)),
            pltpu.SemaphoreType.DMA((SIDE, others)),
            pltpu.SemaphoreType.DMA((ITERS, SIDE, others)),
            pltpu.SemaphoreType.DMA((others,)),
            pltpu.SemaphoreType.DMA((ITERS, others)),
            pltpu.SemaphoreType.DMA((bands - 1,)),
            pltpu.SemaphoreType.DMA((ITERS, bands)),
        ],
        compiler_params=pltpu.CompilerParams(
            collective_id=0, has_side_effects=True, vmem_limit_bytes=52 * 2**20
        ),
        name="both_steps",
    )(*operands)
    return results


def solution(mesh):
    in_specs = (
        P("section", "zone", None, None),
        P("section", "zone"),
        P("section", "zone"),
        P("section", "zone"),
        P(),
        P("section", "zone", None),
        P("section", "zone"),
        P("section", "zone"),
        P("section", "zone", None),
        P("section", "zone", None),
        P("section", "zone", None),
    )
    out_specs = (P("section", "zone", None), P("section", "zone", None), P("section", "zone", None))
    return jax.shard_map(
        per_device, mesh=mesh, in_specs=in_specs, out_specs=out_specs, check_vma=False
    )
```

time: 85.2 us -> 72.5 us (0.85)
  Pallas kernels: 77.6 us -> 68.9 us
  local copies, waits for them, and re-layouts: 6.36 us -> 2.77 us
    pallas_call x2 -> x1, Pallas kernels: 77.6 us -> 68.9 us  [per_device(): pl.pallas_call(steps, out_shape=tuple((pltpu.VMEM(result.shape, F32) for...]
    unnamed x5 -> x3, local copies, waits for them, and re-layouts: 5.19 us -> 2.77 us
    reshape x1 -> x0, local copies, waits for them, and re-layouts: 1.17 us -> none  [per_device(): jnp.pad(block_place, (0, TILE - block_place.shape[0])).reshape(1, TILE)]
where the time goes in v2:
time: 72.5 us; the launch traced here: 72.4 us
  Pallas kernels  68.9 us (95%)
  local copies, waits for them, and re-layouts  2.77 us (4%)
    pallas_call x1, Pallas kernels, per_device(): pl.pallas_call(steps, out_shape=tuple((pltpu.VMEM(result.shape, F32) for...  68.9 us
    unnamed x3, local copies, waits for them, and re-layouts  2.77 us

profile of v2, /device:TPU:1, one launch (start us, length us, event | category | flops | bytes accessed | tf_op | source)
XLA Modules:
  0.0 72.4 jit_solution(3244359363188378544)
XLA Ops:
  0.6 68.9 %both_steps.1 = (f32[1,256,128]{2,1,0:T(8,128)S(1)}, f32[1,2560,128]{2,1,0:T(8,128)S(1)}, f32[1,2560,128]{2,1,0:T(8,128)S(1)}) custom-call(s32[1,64]{1,0:T(1,128)} %bitcast.1, s32[1,128]{1,0:T(1,128)} %tile_row_hbm.1, s32[1,128]{1,0:T(1,128)} %tile_col_hbm.1, s32[1,128]{1,0:T(1,128)} %tile_live_hbm.1, bf16[1,128,128,128]{3,2,1,0:T(8,128)(2,1)} %tiles_hbm.1, ...), custom_call_target="tpu_custom_call" | custom-call | tf_op jit(solution)/shard_map/both_steps/pallas_call | solution.py:509
  69.6 0.7 copy.17
  70.2 1.1 %copy.18 = f32[1,2560,128]{2,1,0:T(8,128)} copy(f32[1,2560,128]{2,1,0:T(8,128)S(1)} %get-tuple-element.4) | data formatting | bytes 2621440
  71.3 1.1 %copy.19 = f32[1,2560,128]{2,1,0:T(8,128)} copy(f32[1,2560,128]{2,1,0:T(8,128)S(1)} %get-tuple-element.5) | data formatting | bytes 2621440

commit v3 on v2

--- a/solution.py
+++ b/solution.py
@@ -14,8 +14,7 @@
 SIDE = 4
 CAP = 4
 TILE = 128
-NEAR_OFFSETS = (2, 1, 3)
-FAR_OFFSETS = (3, 2, 1)
+OFFSETS = (3, 2, 1)
 MESH = pl.DeviceIdType.MESH
 
 F32 = jnp.float32
@@ -85,6 +84,9 @@
     tiles,
     demand,
     flow_cost,
+    flows_in,
+    flows_got,
+    flows_turned,
     stock_cost,
     cost_turned,
     dual_turned,
@@ -97,12 +99,13 @@
     far_send,
     far_got,
     far_own,
-    near_send,
     near_got,
     blocks,
     products,
     running,
     load_sem,
+    flow_send_sem,
+    flow_got_sem,
     x_send_sem,
     x_got_sem,
     pair_send_sem,
@@ -132,12 +135,15 @@
     def own_zone(far_step, near_step):
         return zone_of(far + far_step, near + near_step, core)
 
-    def pair_zone(far_step, near_step):
-        return zone_of(near + far_step, far + near_step, 1 - core)
-
-    pair = pair_zone(0, 0)
-    far_peers = [own_zone(off, 0) for off in FAR_OFFSETS]
-    near_peers = [own_zone(0, off) for off in NEAR_OFFSETS]
+    def own_band(far_step, near_at):
+        return zone_of(far + far_step, near_at, core)
+
+    def pair_band(far_step, near_at):
+        return zone_of(near + far_step, near_at, 1 - core)
+
+    pair = pair_band(0, far)
+    far_peers = [own_zone(off, 0) for off in OFFSETS]
+    near_peers = [own_zone(0, off) for off in OFFSETS]
     section_after = (section + 1) % SIDE
     section_before = (section + SIDE - 1) % SIDE
 
@@ -150,12 +156,12 @@
                 (tile_col_hbm, tile_col),
                 (tile_live_hbm, tile_live),
                 (duals_hbm.at[0], duals),
+                (flow_cost_hbm, flow_cost.at[near]),
+                (flows_hbm.at[0], flows_in),
                 (tiles_hbm.at[0], tiles),
                 (stock_cost_hbm, stock_cost),
-                (flow_cost_hbm, flow_cost),
                 (stock_hbm.at[0], stock),
                 (demand_hbm.at[0], demand),
-                (flows_hbm.at[0], flows),
                 (table_made, table),
             )
         )
@@ -264,52 +270,91 @@
             (section, far_peers[number]),
         )
 
-    def near_copy(it, part):
+    def near_copy(it, part, number):
+        held = near_got.at[it, part, near]
         return remote(
-            near_send.at[part],
-            near_got.at[it, part],
-            near_send_sem.at[part],
-            near_got_sem.at[it, part],
-            (section, near_peers[part]),
-        )
-
-    def pull_for_pair(it, part):
+            held,
+            held,
+            near_send_sem.at[part, number],
+            near_got_sem.at[it, part, near],
+            (section, near_peers[number]),
+        )
+
+    def near_arrival(it, part, number):
+        source = (near + OFFSETS[number]) % SIDE
+        held = near_got.at[it, part, source]
+        return remote(
+            held,
+            held,
+            near_send_sem.at[part, number],
+            near_got_sem.at[it, part, source],
+            (section, pair),
+        )
+
+    def flow_copies(number, source, device):
+        return [
+            remote(
+                ref.at[source],
+                ref.at[source],
+                flow_send_sem.at[which, number],
+                flow_got_sem.at[which, source],
+                (section, device),
+            )
+            for which, ref in enumerate((flows_got, flow_cost))
+        ]
+
+    def pull_for_pair(part):
         def one(number):
-            band = pair_zone(SIDE - 1 - number, (NEAR_OFFSETS + (0,))[part])
+            band = pair_band(SIDE - 1 - number, part)
             first, second = pull_band(band)
             pair_send[part, number, :, :TILE] = first.astype(BF16)
             pair_send[part, number, :, TILE:] = second.astype(BF16)
 
         loop(SIDE, one, 2)
-        pair_copy(it, part).start()
 
     def pull_own(it, part):
         pair_copy(it, part).wait_recv()
         for number in range(SIDE):
-            band = own_zone(SIDE - 1 - number, (NEAR_OFFSETS + (0,))[part])
+            band = own_band(SIDE - 1 - number, part)
             first, second = pull_band(band)
             first = first + pair_got[it, part, number, :, :TILE].astype(F32)
             second = second + pair_got[it, part, number, :, TILE:].astype(F32)
-            if number < len(FAR_OFFSETS):
+            if number < len(OFFSETS):
                 far_send[part, number, :, :TILE] = first.astype(BF16)
                 far_send[part, number, :, TILE:] = second.astype(BF16)
             else:
                 far_own[part, :, :TILE] = first
                 far_own[part, :, TILE:] = second
-        for number in range(len(FAR_OFFSETS)):
+        for number in range(len(OFFSETS)):
             far_copy(it, part, number).start()
 
-    def far_sum(it, part):
-        for number in range(len(FAR_OFFSETS)):
+    def pass_to_near(it, part):
+        for number in range(len(OFFSETS)):
             far_copy(it, part, number).wait_recv()
         total = far_own[part]
-        for number in range(len(FAR_OFFSETS)):
+        for number in range(len(OFFSETS)):
             total = total + far_got[it, part, number].astype(F32)
-        return total
-
-    def pass_to_near(it, part):
-        near_send[part] = far_sum(it, part).astype(BF16)
-        near_copy(it, part).start()
+        near_got[it, part, near] = total.astype(BF16)
+        for number in range(len(OFFSETS)):
+            near_copy(it, part, number).start()
+
+    def step_flows(it, part):
+        for number in range(len(OFFSETS)):
+            near_arrival(it, part, number).wait_recv()
+        pulled = near_got[it, part, 0].astype(F32)
+        for source in range(1, SIDE):
+            pulled = pulled + near_got[it, part, source].astype(F32)
+        held = flows_turned[part]
+        fresh = jnp.maximum(held - STEP_PRIMAL * (flow_cost[part] - pulled), 0.0)
+        flows_turned[part] = fresh
+        bar = (2.0 * fresh - held).astype(BF16)
+        band = own_band(0, part)
+        for block in range(flows.shape[0] // TILE):
+            lanes = slice(block * TILE, (block + 1) * TILE)
+            blocks[it, band, lanes, :] = jnp.transpose(bar[:, lanes])
+        for number in range(len(OFFSETS)):
+            block_copy(it, band, 4 * part + number, far_peers[number]).start()
+        block_copy(it, band, 4 * part + 3, pair).start()
 
     def update_stock(it, chunk):
         dual_copy(it, chunk).wait_recv()
@@ -341,103 +386,120 @@
         load.wait()
     prepare(place, tile_row, tile_col, tile_live, table_made)
     loads[-1].start()
+    loads[4].wait()
+
+    def first_turn(tile):
+        turn(tile, duals[rows_of(tile), :])
+
+    loop(zone_tiles, first_turn, 4)
+    for load in loads[5:7]:
+        load.wait()
+    flows_got[near] = flows_in[...].astype(BF16)
+    loads[-1].wait()
+    loads[7].wait()
+    pull_for_pair(0)
+    pull_for_pair(1)
     pl.semaphore_wait(barrier, len(partners))
-    loads[4].wait()
-    for chunk in range(chunks):
-        def first_turn(step):
-            tile = chunk * chunk_tiles + step
-            turn(tile, duals[rows_of(tile), :])
-
-        loop(chunk_tiles, first_turn, 2)
-        dual_copy(0, chunk).start()
-    loads[6].wait()
-
-    def turn_cost(tile):
-        rows = rows_of(tile)
-        cost_turned[rows, :] = lanes_to_rows(stock_cost[:, rows])
-
-    loop(zone_tiles, turn_cost, 2)
-    loads[-1].wait()
-    loads[5].wait()
-    for load in loads[7:-1]:
-        load.wait()
+
+    def start_flows():
+        for number, peer in enumerate(near_peers):
+            for copy in flow_copies(number, near, peer):
+                copy.start()
+
+    def first_waits():
+        for load in loads[8:-1]:
+            load.wait()
+
+        def turn_cost(tile):
+            rows = rows_of(tile)
+            cost_turned[rows, :] = lanes_to_rows(stock_cost[:, rows])
+
+        loop(zone_tiles, turn_cost, 4)
+
+    def first_flows():
+        for number, off in enumerate(OFFSETS):
+            for copy in flow_copies(number, (near + off) % SIDE, pair):
+                copy.wait_recv()
+
+        def turn_flows(at):
+            for block in range(flows.shape[0] // TILE):
+                lanes = slice(block * TILE, (block + 1) * TILE)
+                flows_turned[at, :, lanes] = jnp.transpose(flows_got[at, lanes, :].astype(F32))
+
+        loop(SIDE, turn_flows, 2)
+        for block in range(flows.shape[0] // TILE):
+            lanes = slice(block * TILE, (block + 1) * TILE)
+            flows_turned[near, :, lanes] = jnp.transpose(flows_in[lanes, :])
+        for number, peer in enumerate(near_peers):
+            for copy in flow_copies(number, near, peer):
+                copy.wait_send()
 
     def iteration(it):
-        pull_for_pair(it, 0)
-        pull_for_pair(it, 1)
+        pair_copy(it, 0).start()
+        pair_copy(it, 1).start()
+        for chunk in range(chunks):
+            dual_copy(it, chunk).start()
+        pl.when(it == 0)(start_flows)
         pull_own(it, 0)
-        pull_for_pair(it, 2)
+        pull_for_pair(2)
+        pair_copy(it, 2).start()
         pull_own(it, 1)
-        pull_for_pair(it, 3)
+        pull_for_pair(3)
+        pair_copy(it, 3).start()
         pull_own(it, 2)
         pull_own(it, 3)
+        pl.when(it == 0)(first_waits)
         update_stock(it, 0)
-        for part in range(len(NEAR_OFFSETS)):
-            pass_to_near(it, part)
-        pulled = far_sum(it, len(NEAR_OFFSETS))
         update_stock(it, 1)
-        for part in range(len(NEAR_OFFSETS)):
-            near_copy(it, part).wait_recv()
-        for part in range(len(NEAR_OFFSETS)):
-            pulled = pulled + near_got[it, part].astype(F32)
-
-        for block in range(flows.shape[0] // TILE):
-            rows = pl.ds(block * TILE, TILE)
-            cost = lanes_to_rows(flow_cost[:, rows])
-            here = jnp.transpose(pulled[:, block * TILE : (block + 1) * TILE])
-            held = flows[rows, :]
-            fresh = jnp.maximum(held - STEP_PRIMAL * (cost - here), 0.0)
-            flows[rows, :] = fresh
-            blocks[it, me, rows, :] = (2.0 * fresh - held).astype(BF16)
+        pass_to_near(it, 0)
+        pass_to_near(it, 1)
+        update_stock(it, 2)
+        pass_to_near(it, 2)
+        pass_to_near(it, 3)
+        update_stock(it, 3)
+        pl.when(it == 0)(first_flows)
+        update_stock(it, 4)
+
+        step_flows(it, 0)
+        update_stock(it, 5)
+        step_flows(it, 1)
+        step_flows(it, 2)
+        update_stock(it, 6)
+        step_flows(it, 3)
+        update_stock(it, 7)
 
         def got(band):
             block_copy(it, band, 0, pair).wait_recv()
 
-        near_order = (1, 3, 2)
-        far_order = (1, 3, 2)
-        for number, step in enumerate(near_order):
-            block_copy(it, me, number, own_zone(0, step)).start()
-        block_copy(it, me, 3, pair).start()
-        for number, step in enumerate(far_order):
-            block_copy(it, me, 4 + number, own_zone(step, 0)).start()
-        push_band(it, me)
-        update_stock(it, 2)
-        for place_in, near_step in enumerate(near_order):
-            band = own_zone(0, near_step)
-            got(band)
-            for number, step in enumerate(far_order):
-                block_copy(it, band, 7 + 4 * place_in + number, own_zone(step, 0)).start()
-            block_copy(it, band, 10 + 4 * place_in, pair).start()
-        loop(SIDE - 1, lambda step: push_band(it, own_zone(0, step + 1)))
-        for near_step in (0,) + near_order:
-            got(pair_zone(0, near_step))
-        loop(SIDE, lambda step: push_band(it, pair_zone(0, step)), 2)
-        update_stock(it, 3)
-
-        def near_of(step):
-            return step + (step // 2) * (1 - 2 * (step % 2))
+        loop(SIDE, lambda step: push_band(it, own_band(0, step)), 2)
+        for part in range(SIDE):
+            got(pair_band(0, part))
+        loop(SIDE, lambda step: push_band(it, pair_band(0, step)), 2)
 
         def own_arrivals(step):
-            for number, far_step in enumerate(far_order):
-                band = own_zone(far_step, near_of(step))
+            for number, far_step in enumerate(OFFSETS):
+                band = own_band(far_step, step)
                 got(band)
-                block_copy(it, band, 19 + 3 * step + number, pair).start()
-            for far_step in far_order:
-                push_band(it, own_zone(far_step, near_of(step)))
+                block_copy(it, band, 4 * SIDE + 3 * step + number, pair).start()
+            for far_step in OFFSETS:
+                push_band(it, own_band(far_step, step))
 
         def pair_arrivals(step):
-            for far_step in far_order:
-                got(pair_zone(far_step, near_of(step)))
-            for far_step in far_order:
-                push_band(it, pair_zone(far_step, near_of(step)))
+            for far_step in OFFSETS:
+                got(pair_band(far_step, step))
+            for far_step in OFFSETS:
+                push_band(it, pair_band(far_step, step))
 
         def both_arrivals(step):
-            own_arrivals(step + 1)
-            pair_arrivals(step)
+            own_arrivals(step + 2)
+            pair_arrivals(step + 1)
 
         own_arrivals(0)
-        update_stock(it, 4)
-        loop(SIDE - 1, both_arrivals)
+        update_stock(it, 8)
+        own_arrivals(1)
+        update_stock(it, 9)
+        pair_arrivals(0)
+        loop(SIDE - 2, both_arrivals)
         pair_arrivals(SIDE - 1)
 
         def accumulate(step, value):
@@ -447,37 +509,55 @@
 
         zero = jnp.zeros((TILE, TILE), F32)
         lax.fori_loop(0, products.shape[0], accumulate, zero, unroll=4)
+        def dual_step(tile, turned):
+            rows = rows_of(tile)
+            pushed = jnp.where(table[6, tile] == 1, running[table[5, tile]], 0.0)
+            pushed = pushed + bar_before[it, rows, :].astype(F32)
+            value = duals[rows, :] - STEP_DUAL * pushed
+            duals[rows, :] = value
+            if turned:
+                turn(tile, value)
+
         for chunk in range(chunks):
             bar_copy(it, chunk).wait_recv()
             dual_copy(it, chunk).wait_send()
-
-            def dual_step(step):
-                tile = chunk * chunk_tiles + step
-                rows = rows_of(tile)
-                pushed = jnp.where(table[6, tile] == 1, running[table[5, tile]], 0.0)
-                pushed = pushed + bar_before[it, rows, :].astype(F32)
-                value = duals[rows, :] - STEP_DUAL * pushed
-                duals[rows, :] = value
-                turn(tile, value)
-
-            loop(chunk_tiles, dual_step, 2)
-
-            @pl.when(it < ITERS - 1)
-            def _():
-                dual_copy(it + 1, chunk).start()
+        for part in range(SIDE):
+            pair_copy(it, part).wait_send()
+
+        @pl.when(it < ITERS - 1)
+        def _():
+            loop(zone_tiles, lambda tile: dual_step(tile, True), 4)
+            pull_for_pair(0)
+            pull_for_pair(1)
+
+        @pl.when(it == ITERS - 1)
+        def _():
+            loop(zone_tiles, lambda tile: dual_step(tile, False), 4)
 
         for chunk in range(chunks):
             bar_copy(it, chunk).wait_send()
         for part in range(SIDE):
-            pair_copy(it, part).wait_send()
-        for part in range(len(NEAR_OFFSETS)):
-            near_copy(it, part).wait_send()
-        for part in range(SIDE):
-            for number in range(len(FAR_OFFSETS)):
+            for number in range(len(OFFSETS)):
                 far_copy(it, part, number).wait_send()
+                near_copy(it, part, number).wait_send()
         loop(block_send_sem.shape[0], lambda number: block_copy(it, me, number, pair).wait_send())
 
     loop(ITERS, iteration)
+    for block in range(flows.shape[0] // TILE):
+        lanes = slice(block * TILE, (block + 1) * TILE)
+        flows[lanes, :] = jnp.transpose(flows_turned[near, :, lanes])
+
+
+def hand_over(*refs):
+    count = len(refs) // 2
+    copies = [
+        pltpu.make_async_copy(refs[number], refs[count + number], refs[-1].at[number])
+        for number in range(count)
+    ]
+    for copy in copies:
+        copy.start()
+    for copy in copies:
+        copy.wait()
 
 
 def per_device(
@@ -499,7 +579,7 @@
     own_flows = flows.shape[1]
     bands = SIDE * SIDE * 2
     others = SIDE - 1
-    chunks = 5
+    chunks = 10
     place_row = block_place.reshape(1, -1)
     anywhere = pl.BlockSpec(memory_space=pl.ANY)
     vmem = pl.BlockSpec(memory_space=pltpu.VMEM)
@@ -520,7 +600,10 @@
             pltpu.SMEM((8, TILE), jnp.int32),
             pltpu.VMEM((slots, TILE, TILE), BF16),
             pltpu.VMEM((zones, TILE), jnp.int32),
-            pltpu.VMEM((1, own_flows), F32),
+            pltpu.VMEM((SIDE, 1, own_flows), F32),
+            pltpu.VMEM((own_flows, TILE), F32),
+            pltpu.VMEM((SIDE, own_flows, TILE), BF16),
+            pltpu.VMEM((SIDE, TILE, own_flows), F32),
             pltpu.VMEM((1, zones), F32),
             pltpu.VMEM((zones, TILE), F32),
             pltpu.VMEM((zone_tiles, TILE, TILE), BF16),
@@ -533,21 +616,22 @@
             pltpu.VMEM((SIDE, others, TILE, own_flows), BF16),
             pltpu.VMEM((ITERS, SIDE, others, TILE, own_flows), BF16),
             pltpu.VMEM((SIDE, TILE, own_flows), F32),
-            pltpu.VMEM((others, TILE, own_flows), BF16),
-            pltpu.VMEM((ITERS, others, TILE, own_flows), BF16),
+            pltpu.VMEM((ITERS, SIDE, SIDE, TILE, own_flows), BF16),
             pltpu.VMEM((ITERS, bands, own_flows, TILE), BF16),
             pltpu.VMEM((bands * CAP, TILE, TILE), F32),
             pltpu.VMEM((bands * CAP, TILE, TILE), F32),
             pltpu.SemaphoreType.DMA((12,)),
+            pltpu.SemaphoreType.DMA((2, others)),
+            pltpu.SemaphoreType.DMA((2, SIDE)),
             pltpu.SemaphoreType.DMA((2, chunks)),
             pltpu.SemaphoreType.DMA((ITERS, 2, chunks)),
             pltpu.SemaphoreType.DMA((SIDE,)),
             pltpu.SemaphoreType.DMA((ITERS, SIDE)),
             pltpu.SemaphoreType.DMA((SIDE, others)),
             pltpu.SemaphoreType.DMA((ITERS, SIDE, others)),
-            pltpu.SemaphoreType.DMA((others,)),
-            pltpu.SemaphoreType.DMA((ITERS, others)),
-            pltpu.SemaphoreType.DMA((bands - 1,)),
+            pltpu.SemaphoreType.DMA((SIDE, others)),
+            pltpu.SemaphoreType.DMA((ITERS, SIDE, SIDE)),
+            pltpu.SemaphoreType.DMA((7 * SIDE,)),
             pltpu.SemaphoreType.DMA((ITERS, bands)),
         ],
         compiler_params=pltpu.CompilerParams(
@@ -555,7 +639,15 @@
         ),
         name="both_steps",
     )(*operands)
-    return results
+    results = [pltpu.with_memory_space_constraint(result, pltpu.VMEM) for result in results]
+    return pl.pallas_call(
+        hand_over,
+        out_shape=tuple(jax.ShapeDtypeStruct(result.shape, F32) for result in results),
+        in_specs=[vmem] * len(results),
+        out_specs=(anywhere,) * len(results),
+        scratch_shapes=[pltpu.SemaphoreType.DMA((len(results),))],
+        name="hand_over",
+    )(*results)
 
 
 def solution(mesh):

time: 72.5 us -> 67.9 us (0.937)
  local copies, waits for them, and re-layouts: 2.77 us -> 0 us
  Pallas kernels: 68.9 us -> 67.1 us
    pallas_call x1, Pallas kernels: 68.9 us -> 65.6 us  [per_device(): pl.pallas_call(steps, out_shape=tuple((pltpu.VMEM(result.shape, F32) for...]
    unnamed x3 -> x0, local copies, waits for them, and re-layouts: 2.77 us -> none
    pallas_call x0 -> x1, Pallas kernels: none -> 1.56 us  [per_device(): pl.pallas_call(hand_over, out_shape=tuple((jax.ShapeDtypeStruct(result.sh...]
where the time goes in v3:
time: 67.9 us; the launch traced here: 67.8 us
  Pallas kernels  67.1 us (99%)
    pallas_call x1, Pallas kernels, per_device(): pl.pallas_call(steps, out_shape=tuple((pltpu.VMEM(result.shape, F32) for...  65.6 us
    pallas_call x1, Pallas kernels, per_device(): pl.pallas_call(hand_over, out_shape=tuple((jax.ShapeDtypeStruct(result.sh...  1.56 us

profile of v3, /device:TPU:1, one launch (start us, length us, event | category | flops | bytes accessed | tf_op | source)
XLA Modules:
  0.0 67.8 jit_solution(6406074606014553303)
XLA Ops:
  0.6 65.6 %both_steps.1 = (f32[1,256,128]{2,1,0:T(8,128)S(1)}, f32[1,2560,128]{2,1,0:T(8,128)S(1)}, f32[1,2560,128]{2,1,0:T(8,128)S(1)}) custom-call(s32[1,64]{1,0:T(1,128)} %bitcast.1, s32[1,128]{1,0:T(1,128)} %tile_row_hbm.1, s32[1,128]{1,0:T(1,128)} %tile_col_hbm.1, s32[1,128]{1,0:T(1,128)} %tile_live_hbm.1, bf16[1,128,128,128]{3,2,1,0:T(8,128)(2,1)} %tiles_hbm.1, ...), custom_call_target="tpu_custom_call" | custom-call | tf_op jit(solution)/shard_map/both_steps/pallas_call | solution.py:589
  66.2 1.6 %hand_over.1 = (f32[1,256,128]{2,1,0:T(8,128)}, f32[1,2560,128]{2,1,0:T(8,128)}, f32[1,2560,128]{2,1,0:T(8,128)}) custom-call(f32[1,256,128]{2,1,0:T(8,128)S(1)} %get-tuple-element.6.refs_0_, f32[1,2560,128]{2,1,0:T(8,128)S(1)} %get-tuple-element.7.refs_1_, f32[1,2560,128]{2,1,0:T(8,128)S(1)} %get-tuple-element.8.refs_2_), custom_call_target="tpu_custom_call" | custom-call | tf_op jit(solution)/shard_map/hand_over/pallas_call | solution.py:643

commit v4 on v3

--- a/solution.py
+++ b/solution.py
@@ -15,6 +15,8 @@
 CAP = 4
 TILE = 128
 OFFSETS = (3, 2, 1)
+SEND_ORDER = (1, 0, 2)
+WAIT_ORDER = (0, 2, 1)
 MESH = pl.DeviceIdType.MESH
 
 F32 = jnp.float32
@@ -310,7 +312,7 @@
             pair_send[part, number, :, :TILE] = first.astype(BF16)
             pair_send[part, number, :, TILE:] = second.astype(BF16)
 
-        loop(SIDE, one, 2)
+        loop(SIDE, one, 4)
 
     def pull_own(it, part):
         pair_copy(it, part).wait_recv()
@@ -325,7 +327,7 @@
             else:
                 far_own[part, :, :TILE] = first
                 far_own[part, :, TILE:] = second
-        for number in range(len(OFFSETS)):
+        for number in SEND_ORDER:
             far_copy(it, part, number).start()
 
     def pass_to_near(it, part):
@@ -335,7 +337,7 @@
         for number in range(len(OFFSETS)):
             total = total + far_got[it, part, number].astype(F32)
         near_got[it, part, near] = total.astype(BF16)
-        for number in range(len(OFFSETS)):
+        for number in SEND_ORDER:
             near_copy(it, part, number).start()
 
     def step_flows(it, part):
@@ -352,7 +354,7 @@
         for block in range(flows.shape[0] // TILE):
             lanes = slice(block * TILE, (block + 1) * TILE)
             blocks[it, band, lanes, :] = jnp.transpose(bar[:, lanes])
-        for number in range(len(OFFSETS)):
+        for number in SEND_ORDER:
             block_copy(it, band, 4 * part + number, far_peers[number]).start()
         block_copy(it, band, 4 * part + 3, pair).start()
 
@@ -471,14 +473,14 @@
         def got(band):
             block_copy(it, band, 0, pair).wait_recv()
 
-        loop(SIDE, lambda step: push_band(it, own_band(0, step)), 2)
+        loop(SIDE, lambda step: push_band(it, own_band(0, step)), 4)
         for part in range(SIDE):
             got(pair_band(0, part))
-        loop(SIDE, lambda step: push_band(it, pair_band(0, step)), 2)
+        loop(SIDE, lambda step: push_band(it, pair_band(0, step)), 4)
 
         def own_arrivals(step):
-            for number, far_step in enumerate(OFFSETS):
-                band = own_band(far_step, step)
+            for number in WAIT_ORDER:
+                band = own_band(OFFSETS[number], step)
                 got(band)
                 block_copy(it, band, 4 * SIDE + 3 * step + number, pair).start()
             for far_step in OFFSETS:
@@ -508,7 +510,7 @@
             return value
 
         zero = jnp.zeros((TILE, TILE), F32)
-        lax.fori_loop(0, products.shape[0], accumulate, zero, unroll=4)
+        lax.fori_loop(0, products.shape[0], accumulate, zero, unroll=8)
         def dual_step(tile, turned):
             rows = rows_of(tile)
             pushed = jnp.where(table[6, tile] == 1, running[table[5, tile]], 0.0)

time: 67.9 us -> 66.1 us (0.973)
  Pallas kernels: 67.1 us -> 65.4 us
    pallas_call x1, Pallas kernels: 65.6 us -> 63.8 us  [per_device(): pl.pallas_call(steps, out_shape=tuple((pltpu.VMEM(result.shape, F32) for...]
where the time goes in v4:
time: 66.1 us; the launch traced here: 66 us
  Pallas kernels  65.4 us (99%)
    pallas_call x1, Pallas kernels, per_device(): pl.pallas_call(steps, out_shape=tuple((pltpu.VMEM(result.shape, F32) for...  63.8 us
    pallas_call x1, Pallas kernels, per_device(): pl.pallas_call(hand_over, out_shape=tuple((jax.ShapeDtypeStruct(result.sh...  1.56 us

profile of v4, /device:TPU:1, one launch (start us, length us, event | category | flops | bytes accessed | tf_op | source)
XLA Modules:
  0.0 66.0 jit_solution(6284535308158471566)
XLA Ops:
  0.6 63.8 %both_steps.1 = (f32[1,256,128]{2,1,0:T(8,128)S(1)}, f32[1,2560,128]{2,1,0:T(8,128)S(1)}, f32[1,2560,128]{2,1,0:T(8,128)S(1)}) custom-call(s32[1,64]{1,0:T(1,128)} %bitcast.1, s32[1,128]{1,0:T(1,128)} %tile_row_hbm.1, s32[1,128]{1,0:T(1,128)} %tile_col_hbm.1, s32[1,128]{1,0:T(1,128)} %tile_live_hbm.1, bf16[1,128,128,128]{3,2,1,0:T(8,128)(2,1)} %tiles_hbm.1, ...), custom_call_target="tpu_custom_call" | custom-call | tf_op jit(solution)/shard_map/both_steps/pallas_call | solution.py:591
  64.5 1.6 %hand_over.1 = (f32[1,256,128]{2,1,0:T(8,128)}, f32[1,2560,128]{2,1,0:T(8,128)}, f32[1,2560,128]{2,1,0:T(8,128)}) custom-call(f32[1,256,128]{2,1,0:T(8,128)S(1)} %get-tuple-element.6.refs_0_, f32[1,2560,128]{2,1,0:T(8,128)S(1)} %get-tuple-element.7.refs_1_, f32[1,2560,128]{2,1,0:T(8,128)S(1)} %get-tuple-element.8.refs_2_), custom_call_target="tpu_custom_call" | custom-call | tf_op jit(solution)/shard_map/hand_over/pallas_call | solution.py:645

commit v5 on v4

--- a/solution.py
+++ b/solution.py
@@ -402,11 +402,13 @@
     pull_for_pair(0)
     pull_for_pair(1)
     pl.semaphore_wait(barrier, len(partners))
-
-    def start_flows():
-        for number, peer in enumerate(near_peers):
-            for copy in flow_copies(number, near, peer):
-                copy.start()
+    pair_copy(0, 0).start()
+    pair_copy(0, 1).start()
+    for chunk in range(chunks):
+        dual_copy(0, chunk).start()
+    for number, peer in enumerate(near_peers):
+        for copy in flow_copies(number, near, peer):
+            copy.start()
 
     def first_waits():
         for load in loads[8:-1]:
@@ -437,11 +439,6 @@
                 copy.wait_send()
 
     def iteration(it):
-        pair_copy(it, 0).start()
-        pair_copy(it, 1).start()
-        for chunk in range(chunks):
-            dual_copy(it, chunk).start()
-        pl.when(it == 0)(start_flows)
         pull_own(it, 0)
         pull_for_pair(2)
         pair_copy(it, 2).start()
@@ -454,21 +451,22 @@
         update_stock(it, 0)
         update_stock(it, 1)
         pass_to_near(it, 0)
+        update_stock(it, 2)
         pass_to_near(it, 1)
-        update_stock(it, 2)
         pass_to_near(it, 2)
+        update_stock(it, 3)
         pass_to_near(it, 3)
-        update_stock(it, 3)
+        update_stock(it, 4)
         pl.when(it == 0)(first_flows)
-        update_stock(it, 4)
+        update_stock(it, 5)
 
         step_flows(it, 0)
-        update_stock(it, 5)
         step_flows(it, 1)
+        update_stock(it, 6)
         step_flows(it, 2)
-        update_stock(it, 6)
+        update_stock(it, 7)
         step_flows(it, 3)
-        update_stock(it, 7)
+        update_stock(it, 8)
 
         def got(band):
             block_copy(it, band, 0, pair).wait_recv()
@@ -497,9 +495,8 @@
             pair_arrivals(step + 1)
 
         own_arrivals(0)
-        update_stock(it, 8)
+        update_stock(it, 9)
         own_arrivals(1)
-        update_stock(it, 9)
         pair_arrivals(0)
         loop(SIDE - 2, both_arrivals)
         pair_arrivals(SIDE - 1)
@@ -529,8 +526,11 @@
         @pl.when(it < ITERS - 1)
         def _():
             loop(zone_tiles, lambda tile: dual_step(tile, True), 4)
-            pull_for_pair(0)
-            pull_for_pair(1)
+            for chunk in range(chunks):
+                dual_copy(it + 1, chunk).start()
+            for part in range(2):
+                pull_for_pair(part)
+                pair_copy(it + 1, part).start()
 
         @pl.when(it == ITERS - 1)
         def _():

time: 66.1 us -> 65.4 us (0.989)
  Pallas kernels: 65.4 us -> 64.6 us
    pallas_call x1, Pallas kernels: 63.8 us -> 63.1 us  [per_device(): pl.pallas_call(steps, out_shape=tuple((pltpu.VMEM(result.shape, F32) for...]
where the time goes in v5:
time: 65.4 us; the launch traced here: 65.3 us
  Pallas kernels  64.6 us (99%)
    pallas_call x1, Pallas kernels, per_device(): pl.pallas_call(steps, out_shape=tuple((pltpu.VMEM(result.shape, F32) for...  63.1 us
    pallas_call x1, Pallas kernels, per_device(): pl.pallas_call(hand_over, out_shape=tuple((jax.ShapeDtypeStruct(result.sh...  1.56 us

profile of v5, /device:TPU:1, one launch (start us, length us, event | category | flops | bytes accessed | tf_op | source)
XLA Modules:
  0.0 65.3 jit_solution(14755367660822243439)
XLA Ops:
  0.6 63.1 %both_steps.1 = (f32[1,256,128]{2,1,0:T(8,128)S(1)}, f32[1,2560,128]{2,1,0:T(8,128)S(1)}, f32[1,2560,128]{2,1,0:T(8,128)S(1)}) custom-call(s32[1,64]{1,0:T(1,128)} %bitcast.1, s32[1,128]{1,0:T(1,128)} %tile_row_hbm.1, s32[1,128]{1,0:T(1,128)} %tile_col_hbm.1, s32[1,128]{1,0:T(1,128)} %tile_live_hbm.1, bf16[1,128,128,128]{3,2,1,0:T(8,128)(2,1)} %tiles_hbm.1, ...), custom_call_target="tpu_custom_call" | custom-call | tf_op jit(solution)/shard_map/both_steps/pallas_call | solution.py:591
  63.7 1.6 %hand_over.1 = (f32[1,256,128]{2,1,0:T(8,128)}, f32[1,2560,128]{2,1,0:T(8,128)}, f32[1,2560,128]{2,1,0:T(8,128)}) custom-call(f32[1,256,128]{2,1,0:T(8,128)S(1)} %get-tuple-element.6.refs_0_, f32[1,2560,128]{2,1,0:T(8,128)S(1)} %get-tuple-element.7.refs_1_, f32[1,2560,128]{2,1,0:T(8,128)S(1)} %get-tuple-element.8.refs_2_), custom_call_target="tpu_custom_call" | custom-call | tf_op jit(solution)/shard_map/hand_over/pallas_call | solution.py:645

commit v6 on v5

--- a/solution.py
+++ b/solution.py
@@ -461,10 +461,10 @@
         update_stock(it, 5)
 
         step_flows(it, 0)
+        update_stock(it, 6)
         step_flows(it, 1)
-        update_stock(it, 6)
+        update_stock(it, 7)
         step_flows(it, 2)
-        update_stock(it, 7)
         step_flows(it, 3)
         update_stock(it, 8)
 

time: 65.4 us -> 65.4 us (level)
  no operation moved by 1% of the time
where the time goes in v6:
time: 65.4 us; the launch traced here: 65.3 us
  Pallas kernels  64.6 us (99%)
    pallas_call x1, Pallas kernels, per_device(): pl.pallas_call(steps, out_shape=tuple((pltpu.VMEM(result.shape, F32) for...  63.1 us
    pallas_call x1, Pallas kernels, per_device(): pl.pallas_call(hand_over, out_shape=tuple((jax.ShapeDtypeStruct(result.sh...  1.56 us

profile of v6, /device:TPU:1, one launch (start us, length us, event | category | flops | bytes accessed | tf_op | source)
XLA Modules:
  0.0 65.3 jit_solution(9304224923872558376)
XLA Ops:
  0.6 63.1 %both_steps.1 = (f32[1,256,128]{2,1,0:T(8,128)S(1)}, f32[1,2560,128]{2,1,0:T(8,128)S(1)}, f32[1,2560,128]{2,1,0:T(8,128)S(1)}) custom-call(s32[1,64]{1,0:T(1,128)} %bitcast.1, s32[1,128]{1,0:T(1,128)} %tile_row_hbm.1, s32[1,128]{1,0:T(1,128)} %tile_col_hbm.1, s32[1,128]{1,0:T(1,128)} %tile_live_hbm.1, bf16[1,128,128,128]{3,2,1,0:T(8,128)(2,1)} %tiles_hbm.1, ...), custom_call_target="tpu_custom_call" | custom-call | tf_op jit(solution)/shard_map/both_steps/pallas_call | solution.py:591
  63.7 1.6 %hand_over.1 = (f32[1,256,128]{2,1,0:T(8,128)}, f32[1,2560,128]{2,1,0:T(8,128)}, f32[1,2560,128]{2,1,0:T(8,128)}) custom-call(f32[1,256,128]{2,1,0:T(8,128)S(1)} %get-tuple-element.6.refs_0_, f32[1,2560,128]{2,1,0:T(8,128)S(1)} %get-tuple-element.7.refs_1_, f32[1,2560,128]{2,1,0:T(8,128)S(1)} %get-tuple-element.8.refs_2_), custom_call_target="tpu_custom_call" | custom-call | tf_op jit(solution)/shard_map/hand_over/pallas_call | solution.py:645
